TPU v7x, 512 devices: a whole 4x8x8 slice. The times are simulated.
512 devices in a mesh: group: 8 (over x, z_lo), space: 64 (over y, z_hi, core).
Axes of the slice: x: 4, y: 8, z: 8 (z_hi: 4, z_lo: 2; z = z_hi * 2 + z_lo), core: 2. Of those that a mesh axis runs over, the one named last changes fastest.
Arguments:
- pressure_prev: float32 [8, 512, 128, 256], P('group', 'space'), may hold values from -6 to 6
- pressure_now: float32 [8, 512, 128, 256], P('group', 'space'), may hold values from -6 to 6
- regions: int32 [512, 128, 256], P('space'), may hold values from 0 to 15
- speed_table: float32 [16], replicated, may hold values from 0.02 to 0.18
- image: float32 [512, 64, 128], P('space', 'group'), may hold values from -6 to 6
- box: int32 [2], replicated, may hold values from 0 to 64, as said below
Outputs:
- out_prev: float32 [8, 512, 128, 256], P('group', 'space')
- out_now: float32 [8, 512, 128, 256], P('group', 'space')
- out_image: float32 [512, 64, 128], P('space', 'group')
Inputs may be any that keep to these rules, and one draw needn't show every extreme that they name: box[0] + 64 <= 128 and box[1] + 128 <= 256; the two entries differ, and one of them equals min(64, 128).
All inputs are finite; a program needn't handle non-finite values.
Results may differ from a plain program's by a relative error of at most 0.00002.
Values sent between devices are 32-bit elements; how exact they have to be, the bound alone decides.
No kernel may reach another device: no remote copies, remote signals or barrier semaphores. Data moves between devices by JAX's collectives and lax.ppermute only.
A program may use at most 64 MiB of HBM per device.

v0:
```python
import jax
import jax.numpy as jnp
from jax import lax
from jax.sharding import PartitionSpec as P

STEPS = 4


coeffs = (-205.0 / 72.0, 8.0 / 5.0, -1.0 / 5.0, 8.0 / 315.0, -1.0 / 560.0)


def padded_2(block, sides, width):
    for axis, dim in sides:
        count = lax.axis_size(axis)
        forward = [(i, i + 1) for i in range(count - 1)]
        backward = [(target, source) for source, target in forward]
        low = lax.ppermute(
            lax.slice_in_dim(block, block.shape[dim] - width, None, axis=dim), axis, forward
        )
        high = lax.ppermute(lax.slice_in_dim(block, 0, width, axis=dim), axis, backward)
        block = jnp.concatenate([low, block, high], axis=dim)
    return block


def laplace(extended):
    rows = extended.shape[0] - 8
    centre = extended[4 : 4 + rows]
    total = 3.0 * coeffs[0] * centre
    for k in range(1, 5):
        total = total + coeffs[k] * (
            extended[4 + k : 4 + k + rows] + extended[4 - k : 4 - k + rows]
        )
    padded = jnp.pad(centre, ((0, 0), (4, 4), (4, 4)))
    ny = centre.shape[1]
    nz = centre.shape[2]
    for k in range(1, 5):
        total = total + coeffs[k] * (
            padded[:, 4 + k : 4 + k + ny, 4 : 4 + nz] + padded[:, 4 - k : 4 - k + ny, 4 : 4 + nz]
        )
        total = total + coeffs[k] * (
            padded[:, 4 : 4 + ny, 4 + k : 4 + k + nz] + padded[:, 4 : 4 + ny, 4 - k : 4 - k + nz]
        )
    return total


def product_groups(received):
    return jnp.prod(received, axis=0)


def local(pressure_prev, pressure_now, regions, speed_table, image, box):
    prev = pressure_prev[0]
    now = pressure_now[0]
    coef = jnp.zeros(now.shape, jnp.float32)
    for region in range(speed_table.shape[0]):
        coef = coef + jnp.where(regions == region, speed_table[region], 0.0)
    zone_y = image.shape[1] * lax.axis_size("group")
    zone_z = image.shape[2]
    planes = now.shape[0]
    total = image
    for step in range(STEPS):
        extended = padded_2(now, (("space", 0),), 4)
        nxt = 2.0 * now - prev + coef * laplace(extended)
        prev, now = (now, nxt)
        zone = lax.dynamic_slice(now, (jnp.int32(0), box[0], box[1]), (planes, zone_y, zone_z))
        total = total + product_groups(
            lax.all_to_all(zone[None], "group", split_axis=2, concat_axis=0, tiled=True)
        )
    return (prev[None], now[None], total)


def solution(mesh):
    placed = (
        P("group", "space", None, None),
        P("group", "space", None, None),
        P("space", None, None),
        P(),
        P("space", "group", None),
        P(),
    )
    return jax.shard_map(
        local,
        mesh=mesh,
        in_specs=placed,
        out_specs=(
            P("group", "space", None, None),
            P("group", "space", None, None),
            P("space", "group", None),
        ),
        check_vma=False,
    )
```

profile of v0, /device:TPU:32, one launch (start us, length us, event | category | flops | bytes accessed | tf_op | source)
XLA Modules:
  0.0 184.7 jit_solution(1637683615906029369)
XLA Ops:
  0.7 1.4 slice_bitcast_fusion.1
  2.1 10.3 %collective-permute-start = (f32[4,128,256]{2,1,0:T(8,128)S(1)}, f32[4,128,256]{2,1,0:T(8,128)S(1)}, u32[]{:S(2)}, u32[]{:S(2)}) collective-permute-start(f32[4,128,256]{2,1,0:T(8,128)S(1)} %get-tuple-element.12), channel_id=1, source_target_pairs={{1,0},{2,1},{3,2},{4,3},{5,4},{6,5},{7,6},{8,7},{9,8},{10,9},{11,1... | collective-permute-start | bytes 1572872 | tf_op jit(solution)/shard_map/ppermute | solution.py:20
  12.4 1.9 %collective-permute-start.1 = (f32[4,128,256]{2,1,0:T(8,128)S(1)}, f32[4,128,256]{2,1,0:T(8,128)S(1)}, u32[]{:S(2)}, u32[]{:S(2)}) collective-permute-start(f32[4,128,256]{2,1,0:T(8,128)S(1)} %get-tuple-element.13), channel_id=1, source_target_pairs={{0,1},{1,2},{2,3},{3,4},{4,5},{5,6},{6,7},{7,8},{8,9},{9,10},{10,1... | collective-permute-start | bytes 1572872 | tf_op jit(solution)/shard_map/ppermute | solution.py:17
  15.0 6.1 %collective-permute-done = f32[4,128,256]{2,1,0:T(8,128)S(1)} collective-permute-done((f32[4,128,256]{2,1,0:T(8,128)S(1)}, f32[4,128,256]{2,1,0:T(8,128)S(1)}, u32[]{:S(2)}, u32[]{:S(2)}) %collective-permute-start) | collective-permute-done | bytes 524320 | tf_op jit(solution)/shard_map/ppermute | solution.py:20
  21.1 11.6 %collective-permute-done.1 = f32[4,128,256]{2,1,0:T(8,128)S(1)} collective-permute-done((f32[4,128,256]{2,1,0:T(8,128)S(1)}, f32[4,128,256]{2,1,0:T(8,128)S(1)}, u32[]{:S(2)}, u32[]{:S(2)}) %collective-permute-start.1) | collective-permute-done | bytes 524320 | tf_op jit(solution)/shard_map/ppermute | solution.py:17
  32.7 17.0 %fusion.92 = f32[8,128,256]{2,1,0:T(8,128)S(1)} fusion(f32[8,128,256]{2,1,0:T(8,128)S(1)} %bitcast.47, f32[4,128,256]{2,1,0:T(8,128)S(1)} %collective-permute-done.1, f32[4,128,256]{2,1,0:T(8,128)S(1)} %collective-permute-done, f32[1,8,128,256]{3,2,1,0:T(8,128)} %param.6, f32[]{:T(128)} %bitcast.17, s32[8,128,256]{2,1,0:T(8,128)S(1)} %copy-done, ...), kind=kLoop, calls=%fused_computation.204 | loop fusion | flops 25165824 | bytes 5242944 | tf_op jit(solution)/shard_map/add | solution.py:62
  49.8 1.9 %collective-permute-start.2 = (f32[4,128,256]{2,1,0:T(8,128)S(1)}, f32[4,128,256]{2,1,0:T(8,128)S(1)}, u32[]{:S(2)}, u32[]{:S(2)}) collective-permute-start(f32[4,128,256]{2,1,0:T(8,128)S(1)} %get-tuple-element.10), channel_id=1, source_target_pairs={{1,0},{2,1},{3,2},{4,3},{5,4},{6,5},{7,6},{8,7},{9,8},{10,9},{11,1... | collective-permute-start | bytes 1572872 | tf_op jit(solution)/shard_map/ppermute | solution.py:20
  51.7 2.4 %collective-permute-start.3 = (f32[4,128,256]{2,1,0:T(8,128)S(1)}, f32[4,128,256]{2,1,0:T(8,128)S(1)}, u32[]{:S(2)}, u32[]{:S(2)}) collective-permute-start(f32[4,128,256]{2,1,0:T(8,128)S(1)} %get-tuple-element.11), channel_id=1, source_target_pairs={{0,1},{1,2},{2,3},{3,4},{4,5},{5,6},{6,7},{7,8},{8,9},{9,10},{10,1... | collective-permute-start | bytes 1572872 | tf_op jit(solution)/shard_map/ppermute | solution.py:17
  54.1 6.8 %collective-permute-done.2 = f32[4,128,256]{2,1,0:T(8,128)S(1)} collective-permute-done((f32[4,128,256]{2,1,0:T(8,128)S(1)}, f32[4,128,256]{2,1,0:T(8,128)S(1)}, u32[]{:S(2)}, u32[]{:S(2)}) %collective-permute-start.2) | collective-permute-done | bytes 524320 | tf_op jit(solution)/shard_map/ppermute | solution.py:20
  60.9 10.8 %collective-permute-done.3 = f32[4,128,256]{2,1,0:T(8,128)S(1)} collective-permute-done((f32[4,128,256]{2,1,0:T(8,128)S(1)}, f32[4,128,256]{2,1,0:T(8,128)S(1)}, u32[]{:S(2)}, u32[]{:S(2)}) %collective-permute-start.3) | collective-permute-done | bytes 524320 | tf_op jit(solution)/shard_map/ppermute | solution.py:17
  71.7 16.0 %fusion.66 = f32[8,128,256]{2,1,0:T(8,128)S(1)} fusion(f32[8,128,256]{2,1,0:T(8,128)S(1)} %fusion.92, f32[4,128,256]{2,1,0:T(8,128)S(1)} %collective-permute-done.3, f32[4,128,256]{2,1,0:T(8,128)S(1)} %collective-permute-done.2, f32[1,8,128,256]{3,2,1,0:T(8,128)S(1)} %copy-done.3, f32[]{:T(128)} %bitcast.17, s32[8,128,256]{2,1,0:T(8,128)S(1)} %copy-done, ...), kind=kLoop, calls=%fused_computation.178 | loop fusion | flops 25165824 | bytes 5242944 | tf_op jit(solution)/shard_map/add | solution.py:62
  87.7 1.1 fusion.180
  88.8 1.9 %collective-permute-start.4 = (f32[4,128,256]{2,1,0:T(8,128)}, f32[4,128,256]{2,1,0:T(8,128)}, u32[]{:S(2)}, u32[]{:S(2)}) collective-permute-start(f32[4,128,256]{2,1,0:T(8,128)} %get-tuple-element.8), channel_id=1, source_target_pairs={{1,0},{2,1},{3,2},{4,3},{5,4},{6,5},{7,6},{8,7},{9,8},{10,9},{11,1... | collective-permute-start | bytes 1572872 | tf_op jit(solution)/shard_map/ppermute | solution.py:20
  90.7 2.4 %collective-permute-start.5 = (f32[4,128,256]{2,1,0:T(8,128)}, f32[4,128,256]{2,1,0:T(8,128)}, u32[]{:S(2)}, u32[]{:S(2)}) collective-permute-start(f32[4,128,256]{2,1,0:T(8,128)} %get-tuple-element.9), channel_id=1, source_target_pairs={{0,1},{1,2},{2,3},{3,4},{4,5},{5,6},{6,7},{7,8},{8,9},{9,10},{10,1... | collective-permute-start | bytes 1572872 | tf_op jit(solution)/shard_map/ppermute | solution.py:17
  98.4 4.5 %all-to-all-start = ((f32[1,8,64,128]{3,1,0,2:T(8,128)}), f32[1,8,64,128]{3,1,0,2:T(8,128)S(1)}, u32[]{:S(2)}, u32[]{:S(2)}) async-start(f32[1,8,64,128]{3,1,0,2:T(8,128)} %bitcast.51), calls=%async_computation | async-start | bytes 524288 | tf_op jit(solution)/shard_map/all_to_all | solution.py:66
  102.9 7.8 %collective-permute-done.5 = f32[4,128,256]{2,1,0:T(8,128)} collective-permute-done((f32[4,128,256]{2,1,0:T(8,128)}, f32[4,128,256]{2,1,0:T(8,128)}, u32[]{:S(2)}, u32[]{:S(2)}) %collective-permute-start.5) | collective-permute-done | bytes 524320 | tf_op jit(solution)/shard_map/ppermute | solution.py:17
  110.7 15.9 %fusion.40 = f32[8,128,256]{2,1,0:T(8,128)S(1)} fusion(f32[8,128,256]{2,1,0:T(8,128)S(1)} %fusion.66, f32[4,128,256]{2,1,0:T(8,128)} %collective-permute-done.5, f32[4,128,256]{2,1,0:T(8,128)} %collective-permute-done.4, f32[8,128,256]{2,1,0:T(8,128)S(1)} %fusion.92, f32[]{:T(128)} %bitcast.17, s32[8,128,256]{2,1,0:T(8,128)S(1)} %copy-done, f32[]{:T(128)} %bitcast.16, ...), kind=kLoop, calls=%fused_computation.152 | loop fusion | flops 25165824 | bytes 5242944 | tf_op jit(solution)/shard_map/add | solution.py:62
  126.7 1.2 fusion.179
  128.0 2.0 %collective-permute-start.6 = (f32[4,128,256]{2,1,0:T(8,128)}, f32[4,128,256]{2,1,0:T(8,128)}, u32[]{:S(2)}, u32[]{:S(2)}) collective-permute-start(f32[4,128,256]{2,1,0:T(8,128)} %get-tuple-element.6), channel_id=1, source_target_pairs={{1,0},{2,1},{3,2},{4,3},{5,4},{6,5},{7,6},{8,7},{9,8},{10,9},{11,1... | collective-permute-start | bytes 1572872 | tf_op jit(solution)/shard_map/ppermute | solution.py:20
  130.0 2.4 %collective-permute-start.7 = (f32[4,128,256]{2,1,0:T(8,128)}, f32[4,128,256]{2,1,0:T(8,128)}, u32[]{:S(2)}, u32[]{:S(2)}) collective-permute-start(f32[4,128,256]{2,1,0:T(8,128)} %get-tuple-element.7), channel_id=1, source_target_pairs={{0,1},{1,2},{2,3},{3,4},{4,5},{5,6},{6,7},{7,8},{8,9},{9,10},{10,1... | collective-permute-start | bytes 1572872 | tf_op jit(solution)/shard_map/ppermute | solution.py:17
  132.6 0.9 copy.32
  133.5 4.3 %all-to-all-start.1 = ((f32[1,8,64,128]{3,1,0,2:T(8,128)}), f32[1,8,64,128]{3,1,0,2:T(8,128)}, u32[]{:S(2)}, u32[]{:S(2)}) async-start(f32[1,8,64,128]{3,1,0,2:T(8,128)} %bitcast.53), calls=%async_computation.1 | async-start | bytes 524288 | tf_op jit(solution)/shard_map/all_to_all | solution.py:66
  137.9 0.9 copy.31
  138.8 6.5 %all-to-all-done.1 = f32[1,8,64,128]{3,1,0,2:T(8,128)} async-done(((f32[1,8,64,128]{3,1,0,2:T(8,128)}), f32[1,8,64,128]{3,1,0,2:T(8,128)}, u32[]{:S(2)}, u32[]{:S(2)}) %all-to-all-start.1) | async-done | bytes 262176 | tf_op jit(solution)/shard_map/all_to_all | solution.py:66
  145.3 6.8 %all-to-all-start.2 = ((f32[1,8,64,128]{3,1,0,2:T(8,128)}), f32[1,8,64,128]{3,1,0,2:T(8,128)}, u32[]{:S(2)}, u32[]{:S(2)}) async-start(f32[1,8,64,128]{3,1,0,2:T(8,128)} %bitcast.50), calls=%async_computation.2 | async-start | bytes 524288 | tf_op jit(solution)/shard_map/all_to_all | solution.py:66
  152.1 15.9 %fusion.14 = f32[8,128,256]{2,1,0:T(8,128)S(1)} fusion(f32[8,128,256]{2,1,0:T(8,128)S(1)} %copy-done.2, f32[4,128,256]{2,1,0:T(8,128)} %collective-permute-done.7, f32[4,128,256]{2,1,0:T(8,128)} %collective-permute-done.6, f32[8,128,256]{2,1,0:T(8,128)S(1)} %fusion.66, f32[]{:T(128)} %bitcast.17, s32[8,128,256]{2,1,0:T(8,128)S(1)} %copy-done, f32[]{:T(128)} %bitcast.16, ...), kind=kLoop, calls=%fused_computation.126 | loop fusion | flops 25165824 | bytes 5242944 | tf_op jit(solution)/shard_map/add | solution.py:62
  168.1 1.0 copy-done.4
  169.2 0.9 copy.30
  170.1 5.7 %all-to-all-start.3 = ((f32[1,8,64,128]{3,1,0,2:T(8,128)}), f32[1,8,64,128]{3,1,0,2:T(8,128)S(1)}, u32[]{:S(2)}, u32[]{:S(2)}) async-start(f32[1,8,64,128]{3,1,0,2:T(8,128)} %bitcast.42), calls=%async_computation.3 | async-start | bytes 524288 | tf_op jit(solution)/shard_map/all_to_all | solution.py:66
  175.8 1.0 reduce_prod.37
  176.8 1.0 reduce_prod.38
  177.7 6.3 %all-to-all-done.3 = f32[1,8,64,128]{3,1,0,2:T(8,128)S(1)} async-done(((f32[1,8,64,128]{3,1,0,2:T(8,128)}), f32[1,8,64,128]{3,1,0,2:T(8,128)S(1)}, u32[]{:S(2)}, u32[]{:S(2)}) %all-to-all-start.3) | async-done | bytes 262176 | tf_op jit(solution)/shard_map/all_to_all | solution.py:66
  (32 shorter events, 3.7 us)
Async XLA Ops:
  0.6 32.1 %copy-start.3 = (f32[1,8,128,256]{3,2,1,0:T(8,128)S(1)}, f32[1,8,128,256]{3,2,1,0:T(8,128)}, u32[]{:S(2)}) copy-start(f32[1,8,128,256]{3,2,1,0:T(8,128)} %param.7) | copy-start | bytes 3145732
  0.6 13.6 %copy-start.5 = (f32[16]{0:T(128)S(1)}, f32[16]{0:T(128)}, u32[]{:S(2)}) copy-start(f32[16]{0:T(128)} %param.9) | copy-start | bytes 196
  0.7 32.0 %copy-start = (s32[8,128,256]{2,1,0:T(8,128)S(1)}, s32[8,128,256]{2,1,0:T(8,128)}, u32[]{:S(2)}) copy-start(s32[8,128,256]{2,1,0:T(8,128)} %param.8) | copy-start | bytes 3145732
  2.1 19.1 %collective-permute-start = (f32[4,128,256]{2,1,0:T(8,128)S(1)}, f32[4,128,256]{2,1,0:T(8,128)S(1)}, u32[]{:S(2)}, u32[]{:S(2)}) collective-permute-start(f32[4,128,256]{2,1,0:T(8,128)S(1)} %get-tuple-element.12), channel_id=1, source_target_pairs={{1,0},{2,1},{3,2},{4,3},{5,4},{6,5},{7,6},{8,7},{9,8},{10,9},{11,1... | collective-permute-start | bytes 1572872 | tf_op jit(solution)/shard_map/ppermute | solution.py:20
  12.4 20.3 %collective-permute-start.1 = (f32[4,128,256]{2,1,0:T(8,128)S(1)}, f32[4,128,256]{2,1,0:T(8,128)S(1)}, u32[]{:S(2)}, u32[]{:S(2)}) collective-permute-start(f32[4,128,256]{2,1,0:T(8,128)S(1)} %get-tuple-element.13), channel_id=1, source_target_pairs={{0,1},{1,2},{2,3},{3,4},{4,5},{5,6},{6,7},{7,8},{8,9},{9,10},{10,1... | collective-permute-start | bytes 1572872 | tf_op jit(solution)/shard_map/ppermute | solution.py:17
  49.8 11.1 %collective-permute-start.2 = (f32[4,128,256]{2,1,0:T(8,128)S(1)}, f32[4,128,256]{2,1,0:T(8,128)S(1)}, u32[]{:S(2)}, u32[]{:S(2)}) collective-permute-start(f32[4,128,256]{2,1,0:T(8,128)S(1)} %get-tuple-element.10), channel_id=1, source_target_pairs={{1,0},{2,1},{3,2},{4,3},{5,4},{6,5},{7,6},{8,7},{9,8},{10,9},{11,1... | collective-permute-start | bytes 1572872 | tf_op jit(solution)/shard_map/ppermute | solution.py:20
  51.7 20.0 %collective-permute-start.3 = (f32[4,128,256]{2,1,0:T(8,128)S(1)}, f32[4,128,256]{2,1,0:T(8,128)S(1)}, u32[]{:S(2)}, u32[]{:S(2)}) collective-permute-start(f32[4,128,256]{2,1,0:T(8,128)S(1)} %get-tuple-element.11), channel_id=1, source_target_pairs={{0,1},{1,2},{2,3},{3,4},{4,5},{5,6},{6,7},{7,8},{8,9},{9,10},{10,1... | collective-permute-start | bytes 1572872 | tf_op jit(solution)/shard_map/ppermute | solution.py:17
  87.7 5.4 %copy-start.7 = (s32[2]{0:T(128)S(1)}, s32[2]{0:T(128)}, u32[]{:S(2)}) copy-start(s32[2]{0:T(128)} %param.11) | copy-start | bytes 28
  88.8 14.1 %collective-permute-start.4 = (f32[4,128,256]{2,1,0:T(8,128)}, f32[4,128,256]{2,1,0:T(8,128)}, u32[]{:S(2)}, u32[]{:S(2)}) collective-permute-start(f32[4,128,256]{2,1,0:T(8,128)} %get-tuple-element.8), channel_id=1, source_target_pairs={{1,0},{2,1},{3,2},{4,3},{5,4},{6,5},{7,6},{8,7},{9,8},{10,9},{11,1... | collective-permute-start | bytes 1572872 | tf_op jit(solution)/shard_map/ppermute | solution.py:20
  90.7 20.0 %collective-permute-start.5 = (f32[4,128,256]{2,1,0:T(8,128)}, f32[4,128,256]{2,1,0:T(8,128)}, u32[]{:S(2)}, u32[]{:S(2)}) collective-permute-start(f32[4,128,256]{2,1,0:T(8,128)} %get-tuple-element.9), channel_id=1, source_target_pairs={{0,1},{1,2},{2,3},{3,4},{4,5},{5,6},{6,7},{7,8},{8,9},{9,10},{10,1... | collective-permute-start | bytes 1572872 | tf_op jit(solution)/shard_map/ppermute | solution.py:17
  98.4 35.1 %all-to-all-start = ((f32[1,8,64,128]{3,1,0,2:T(8,128)}), f32[1,8,64,128]{3,1,0,2:T(8,128)S(1)}, u32[]{:S(2)}, u32[]{:S(2)}) async-start(f32[1,8,64,128]{3,1,0,2:T(8,128)} %bitcast.51), calls=%async_computation | async-start | bytes 524288 | tf_op jit(solution)/shard_map/all_to_all | solution.py:66
  126.7 1.3 copy-start.1
  128.0 9.8 %copy-start.2 = (f32[8,128,256]{2,1,0:T(8,128)S(1)}, f32[8,128,256]{2,1,0:T(8,128)}, u32[]{:S(2)}) copy-start(f32[8,128,256]{2,1,0:T(8,128)} %copy-done.1) | copy-start | bytes 3145732
  128.0 24.1 %collective-permute-start.6 = (f32[4,128,256]{2,1,0:T(8,128)}, f32[4,128,256]{2,1,0:T(8,128)}, u32[]{:S(2)}, u32[]{:S(2)}) collective-permute-start(f32[4,128,256]{2,1,0:T(8,128)} %get-tuple-element.6), channel_id=1, source_target_pairs={{1,0},{2,1},{3,2},{4,3},{5,4},{6,5},{7,6},{8,7},{9,8},{10,9},{11,1... | collective-permute-start | bytes 1572872 | tf_op jit(solution)/shard_map/ppermute | solution.py:20
  130.0 22.1 %collective-permute-start.7 = (f32[4,128,256]{2,1,0:T(8,128)}, f32[4,128,256]{2,1,0:T(8,128)}, u32[]{:S(2)}, u32[]{:S(2)}) collective-permute-start(f32[4,128,256]{2,1,0:T(8,128)} %get-tuple-element.7), channel_id=1, source_target_pairs={{0,1},{1,2},{2,3},{3,4},{4,5},{5,6},{6,7},{7,8},{8,9},{9,10},{10,1... | collective-permute-start | bytes 1572872 | tf_op jit(solution)/shard_map/ppermute | solution.py:17
  133.5 11.9 %all-to-all-start.1 = ((f32[1,8,64,128]{3,1,0,2:T(8,128)}), f32[1,8,64,128]{3,1,0,2:T(8,128)}, u32[]{:S(2)}, u32[]{:S(2)}) async-start(f32[1,8,64,128]{3,1,0,2:T(8,128)} %bitcast.53), calls=%async_computation.1 | async-start | bytes 524288 | tf_op jit(solution)/shard_map/all_to_all | solution.py:66
  145.3 24.7 %all-to-all-start.2 = ((f32[1,8,64,128]{3,1,0,2:T(8,128)}), f32[1,8,64,128]{3,1,0,2:T(8,128)}, u32[]{:S(2)}, u32[]{:S(2)}) async-start(f32[1,8,64,128]{3,1,0,2:T(8,128)} %bitcast.50), calls=%async_computation.2 | async-start | bytes 524288 | tf_op jit(solution)/shard_map/all_to_all | solution.py:66
  168.1 1.0 copy-start.4
  169.2 14.9 %copy-start.6 = (f32[8,8,128]{2,1,0:T(8,128)S(1)}, f32[8,8,128]{2,1,0:T(8,128)}, u32[]{:S(2)}) copy-start(f32[8,8,128]{2,1,0:T(8,128)} %param.10) | copy-start | bytes 98308
  170.1 14.0 %all-to-all-start.3 = ((f32[1,8,64,128]{3,1,0,2:T(8,128)}), f32[1,8,64,128]{3,1,0,2:T(8,128)S(1)}, u32[]{:S(2)}, u32[]{:S(2)}) async-start(f32[1,8,64,128]{3,1,0,2:T(8,128)} %bitcast.42), calls=%async_computation.3 | async-start | bytes 524288 | tf_op jit(solution)/shard_map/all_to_all | solution.py:66
where the time goes:
time: 186 us; the launch traced here: 185 us
  other arithmetic  66.9 us (36%)
  waiting for transfers between devices  55.9 us (30%)
  starting transfers between devices  46.6 us (25%)
  local copies, waits for them, and re-layouts  10.8 us (6%)
  between operations  4.53 us (2%)
    add x4, other arithmetic, local(): nxt = 2.0 * now - prev + coef * laplace(extended)  64.9 us
    ppermute x4, waiting for transfers between devices, padded_2(): lax.ppermute(lax.slice_in_dim(block, block.shape[dim] - width, None, axis...  30.2 us
    all_to_all x4, starting transfers between devices, local(): lax.all_to_all(zone[None], 'group', split_axis=2, concat_axis=0, tiled=True)  21.3 us
    ppermute x4, starting transfers between devices, padded_2(): lax.ppermute(lax.slice_in_dim(block, 0, width, axis=dim), axis, backward)  16.1 us
    ppermute x4, waiting for transfers between devices, padded_2(): lax.ppermute(lax.slice_in_dim(block, 0, width, axis=dim), axis, backward)  12.9 us
    all_to_all x4, waiting for transfers between devices, local(): lax.all_to_all(zone[None], 'group', split_axis=2, concat_axis=0, tiled=True)  12.8 us
    ppermute x4, starting transfers between devices, padded_2(): lax.ppermute(lax.slice_in_dim(block, block.shape[dim] - width, None, axis...  9.14 us
    dynamic_slice x8, local copies, waits for them, and re-layouts, local(): lax.dynamic_slice(now, (jnp.int32(0), box[0], box[1]), (planes, zone_y, z...  4.02 us
  transfers between devices with their start and end apart: 12, of which 7 were waited for; matrix products, arithmetic and copies ran while one was open for 22% of the time, Pallas kernels for 0%

commit v1 on v0

v1 whole, which is shorter than its diff:
```python
import functools

import jax
import jax.numpy as jnp
from jax import lax
from jax.experimental import pallas as pl
from jax.experimental.pallas import tpu as pltpu
from jax.sharding import PartitionSpec as P

STEPS = 4
SCALE = 5040.0
CENTRE = -3.0 * 14350.0
TAPS = (8064.0, -1008.0, 128.0, -9.0)
PLANES, NY, NZ = 8, 128, 256
FACE = 4
HALVES = 2
ROWS = NY // HALVES
ZY, ZZ = 64, 128
GROUPS = 8
VMEM_LIMIT = 16 * 1024 * 1024
COST = (1, 10**10, 1, 10**10)
F32 = jnp.float32
BF16 = jnp.bfloat16

VM = pl.BlockSpec(memory_space=pltpu.VMEM)
SM = pl.BlockSpec(memory_space=pltpu.SMEM)
ANY = pl.BlockSpec(memory_space=pl.ANY)


def band(size):
    apart = jnp.abs(
        lax.broadcasted_iota(jnp.int32, (size, size), 0)
        - lax.broadcasted_iota(jnp.int32, (size, size), 1)
    )
    matrix = jnp.zeros((size, size), F32)
    for k, tap in enumerate(TAPS, 1):
        matrix = jnp.where(apart == k, tap, matrix)
    return matrix.astype(BF16)


def store_bands(across_y, across_z):
    along_y, along_z = band(NY), band(NZ)
    for i in range(3):
        across_y[:, i * NY : (i + 1) * NY] = along_y
        across_z[i * NZ : (i + 1) * NZ, :] = along_z


def call(kernel, outs, in_specs, out_specs, args, cost=1, scratch=(), aliases=None):
    return pl.pallas_call(
        kernel,
        out_shape=[jax.ShapeDtypeStruct(shape, F32) for shape in outs],
        in_specs=in_specs,
        out_specs=out_specs,
        scratch_shapes=list(scratch),
        input_output_aliases=aliases or {},
        compiler_params=pltpu.CompilerParams(vmem_limit_bytes=VMEM_LIMIT),
        cost_estimate=pl.CostEstimate(flops=cost, bytes_accessed=cost, transcendentals=0),
    )(*args)


def thirds(x):
    high = x.astype(BF16)
    left = x - high.astype(F32)
    middle = left.astype(BF16)
    low = (left - middle.astype(F32)).astype(BF16)
    return high, middle, low


def cross_terms(plane, across_y, across_z):
    pieces = thirds(plane)
    along_z = jnp.dot(
        jnp.concatenate(pieces, axis=1), across_z, preferred_element_type=F32
    )
    along_y = jnp.dot(
        across_y, jnp.concatenate(pieces, axis=0), preferred_element_type=F32
    )
    return along_z + along_y


def advance(now, older, coef_of, cross, store_base, store_next):
    for half in range(HALVES):

        @pl.loop(0, ROWS // 8)
        def _(block):
            inner = pl.ds(pl.multiple_of(block * 8, 8), 8)
            outer = pl.ds(pl.multiple_of(half * ROWS + block * 8, 8), 8)
            at = (inner, outer, half)
            values = [now(j, at) for j in range(PLANES)]
            for j in range(PLANES):
                total = cross[j, outer, :] + CENTRE * values[j]
                for k, tap in enumerate(TAPS, 1):
                    pair = [values[i] for i in (j + k, j - k) if 0 <= i < len(values)]
                    if pair:
                        total = total + tap * sum(pair[1:], pair[0])
                value = 2.0 * values[j] - older(j, at) + coef_of(j, at) * total
                if j < FACE:
                    store_base(j, at, value)
                else:
                    store_next(j - FACE, at, value)


def from_natural(ref, flip):
    return lambda j, at: ref[j ^ flip, at[1], :]


def from_parts(first, second, rest):
    def rows(j, at):
        if j >= FACE:
            return rest[j - FACE, at[1], :]
        return (first, second)[at[2]][j, at[0], :]

    return rows


def whole_plane(first, second, rest, j):
    if j >= FACE:
        return rest[j - FACE]
    return jnp.concatenate([first[j], second[j]], axis=0)


def cut_zone(plane, box):
    moved = pltpu.roll(plane, (NY - box[0]) % NY, 0)[:ZY]
    return pltpu.roll(moved, (NZ - box[1]) % NZ, 1)[:, :ZZ]


def split_zone(plane, box):
    return cut_zone(plane, box).reshape(GROUPS, ZY // GROUPS, ZZ)


def put_rows(ref):
    def put(j, at, value):
        ref[j, at[1], :] = value

    return put


def first_kernel(place, table, now, prev, regions, coef, base, rest, cross, across_y, across_z):
    flip = place[0]
    store_bands(across_y, across_z)
    scaled = [table[i] * (1.0 / SCALE) for i in range(16)]
    for j in range(PLANES):
        cross[j] = cross_terms(now[j ^ flip], across_y[...], across_z[...])

    def coef_of(j, at):
        code = regions[j ^ flip, at[1], :]
        level = scaled
        for bit in range(4):
            odd = (code & (1 << bit)) != 0
            level = [
                jnp.where(odd, level[2 * i + 1], level[2 * i]) for i in range(len(level) // 2)
            ]
        coef[j, at[1], :] = level[0]
        return level[0]

    advance(
        from_natural(now, flip),
        from_natural(prev, flip),
        coef_of,
        cross,
        put_rows(base),
        put_rows(rest),
    )


def middle_kernel(first, place, box, n1, n2, partial, halo, *refs):
    *refs, now, base, nxt, zones, cross, across_y, across_z = refs
    if first:
        prev, coef = refs
        older = from_natural(prev, place[0])
        earlier = ()
    else:
        p1, p2, pa, coef, *earlier = refs
        older = from_parts(p1, p2, pa)
    for zone in earlier:
        zones[:, : zone.shape[1]] = zone[...]
    far_terms(coef, partial, halo, 3 - place[1] if first else 0, now)
    store_bands(across_y, across_z)
    for j in range(PLANES):
        plane = whole_plane(n1, n2, now, j)
        cross[j] = cross_terms(plane, across_y[...], across_z[...])
        zones[:, zones.shape[1] - 1, j] = split_zone(plane, box)
    advance(
        from_parts(n1, n2, now),
        older,
        lambda j, at: coef[j, at[1], :],
        cross,
        put_rows(base),
        put_rows(nxt),
    )


def face_terms(base, coef, halo, turn, half, put):
    @pl.loop(0, ROWS // 8)
    def _(block):
        inner = pl.ds(pl.multiple_of(block * 8, 8), 8)
        outer = pl.ds(pl.multiple_of(half * ROWS + block * 8, 8), 8)
        beyond = [halo[k ^ turn, inner, :] for k in range(FACE)]
        for j in range(FACE):
            total = TAPS[j] * beyond[0]
            for k in range(1, FACE - j):
                total = total + TAPS[j + k] * beyond[k]
            put(j, inner, base[j, outer, :] + coef[j, outer, :] * total)


def face_kernel(half, first, place, base, coef, halo, *refs):
    out = refs[2 if half else 0]
    turn = 3 - place[1] if first else 0

    def put(j, inner, value):
        out[j, inner, :] = value

    face_terms(base, coef, halo, turn, half, put)


def far_terms(coef, partial, halo, turn, out):
    @pl.loop(0, NY // 8)
    def _(block):
        rows = pl.ds(pl.multiple_of(block * 8, 8), 8)
        beyond = [halo[(FACE - 1 - k) ^ turn, rows, :] for k in range(FACE)]
        for j in range(FACE):
            total = TAPS[j] * beyond[0]
            for k in range(1, FACE - j):
                total = total + TAPS[j + k] * beyond[k]
            mine = FACE - 1 - j
            out[mine, rows, :] = partial[mine, rows, :] + coef[FACE + mine, rows, :] * total


def last_kernel(box, base, coef, halo, n1, partial, far_halo, earlier, n2, now, zones):
    def put(j, inner, value):
        n2[j, inner, :] = value

    face_terms(base, coef, halo, 0, 1, put)
    far_terms(coef, partial, far_halo, 0, now)
    zones[:, : STEPS - 1] = earlier[...]
    for j in range(PLANES):
        zones[:, STEPS - 1, j] = split_zone(whole_plane(n1, n2, now, j), box)


def gather_kernel(place, n1, n2, na, out, sems):
    flip = place[0]
    copies = []
    for j in range(FACE):
        copies.append((n1.at[j], out.at[j ^ flip, pl.ds(0, ROWS)]))
        copies.append((n2.at[j], out.at[j ^ flip, pl.ds(ROWS, ROWS)]))
        copies.append((na.at[j], out.at[(j + FACE) ^ flip]))
    copies = [
        pltpu.make_async_copy(source, target, sems.at[i])
        for i, (source, target) in enumerate(copies)
    ]
    for copy in copies:
        copy.start()
    for copy in copies:
        copy.wait()


def image_kernel(place, image, received, out):
    for j in range(PLANES):
        at = j ^ place[0]
        total = image[at]
        for step in range(received.shape[1]):
            product = received[0, step, j]
            for group in range(1, GROUPS):
                product = product * received[group, step, j]
            total = total + product
        out[at] = total


def local(pressure_prev, pressure_now, regions, speed_table, image, box):
    prev = pressure_prev[0]
    now = pressure_now[0]
    odd = lax.rem(lax.axis_index("space"), 2)
    place = jnp.stack([7 * odd, 3 * odd]).astype(jnp.int32)
    count = lax.axis_size("space")
    inside = [(i, i ^ 1) for i in range(count)]
    across = [(i, i + 1) for i in range(1, count - 1, 2)]
    across = across + [(j, i) for i, j in across]
    half_shape = (FACE, ROWS, NZ)
    face_shape = (FACE, NY, NZ)
    slab_shape = (PLANES, NY, NZ)
    zone_rows = (ZY // GROUPS, ZZ)
    slab = pltpu.VMEM(slab_shape, F32)
    work = [slab, pltpu.VMEM((NY, 3 * NY), BF16), pltpu.VMEM((3 * NZ, NZ), BF16)]

    def swap_faces(halves):
        return [lax.ppermute(half, "space", across) for half in halves]

    beyond = swap_faces(
        lax.dynamic_slice(now, (4 * odd, half * ROWS, 0), half_shape) for half in range(HALVES)
    )
    halo = lax.ppermute(
        lax.dynamic_slice(now, (4 - 4 * odd, 0, 0), face_shape), "space", inside
    )
    coef, base, rest = call(
        first_kernel,
        [slab_shape] + [face_shape] * 2,
        [SM, SM] + [VM] * 3,
        [VM] * 3,
        (place, speed_table, now, prev, regions),
        scratch=work,
    )
    older = [now]
    zones = ()
    for step in range(STEPS - 1):
        n1 = call(
            functools.partial(face_kernel, 0, step == 0),
            [half_shape],
            [SM] + [VM] * 3,
            [VM],
            (place, base, coef, beyond[0]),
        )[0]
        n2, rest = call(
            functools.partial(face_kernel, 1, step == 0),
            [half_shape, face_shape],
            [SM] + [VM] * 3 + [ANY] * 2,
            [VM, ANY],
            (place, base, coef, beyond[1], rest, n1),
            cost=COST[1],
            aliases={4: 1},
        )
        beyond = swap_faces([n1, n2])
        full, base, rest, zone = call(
            functools.partial(middle_kernel, step == 0),
            [face_shape] * 3 + [(GROUPS, step + 1, PLANES) + zone_rows],
            [SM, SM] + [VM] * (5 + len(older) + len(zones)),
            [VM] * 4,
            (place, box, n1, n2, rest, halo, *older, coef, *zones),
            cost=COST[0] if step < STEPS - 2 else COST[2],
            scratch=work,
        )
        zones = (zone,)
        older = (n1, n2, full)
        halo = lax.ppermute(full, "space", inside)
    n1 = call(
        functools.partial(face_kernel, 0, False),
        [half_shape],
        [SM] + [VM] * 3,
        [VM],
        (place, base, coef, beyond[0]),
        cost=COST[3],
    )[0]
    n2, full, zone = call(
        last_kernel,
        [half_shape, face_shape, (GROUPS, STEPS, PLANES) + zone_rows],
        [SM] + [VM] * 7,
        [VM] * 3,
        (box, base, coef, beyond[1], n1, rest, halo, zone),
    )
    received = lax.all_to_all(zone, "group", split_axis=0, concat_axis=0, tiled=True)

    def gather(three):
        return call(
            gather_kernel,
            [slab_shape],
            [SM] + [ANY] * 3,
            [ANY],
            (place, *three),
            scratch=[pltpu.SemaphoreType.DMA((12,))],
        )[0]

    out_prev = gather(older)
    out_now = gather((n1, n2, full))
    total = call(
        image_kernel, [image.shape], [SM] + [VM] * 2, [VM], (place, image, received)
    )[0]
    return (out_prev[None], out_now[None], total)


def solution(mesh):
    placed = (
        P("group", "space", None, None),
        P("group", "space", None, None),
        P("space", None, None),
        P(),
        P("space", "group", None),
        P(),
    )
    return jax.shard_map(
        local,
        mesh=mesh,
        in_specs=placed,
        out_specs=(
            P("group", "space", None, None),
            P("group", "space", None, None),
            P("space", "group", None),
        ),
        check_vma=False,
    )
```

time: 186 us -> 99.1 us (0.53)
  other arithmetic: 66.9 us -> 0.08 us
  waiting for transfers between devices: 55.9 us -> 16.3 us
  Pallas kernels: 0 us -> 21.1 us
  starting transfers between devices: 46.6 us -> 55.5 us
  local copies, waits for them, and re-layouts: 10.8 us -> 4.65 us
  between operations: 4.53 us -> 0.97 us
    add x5 -> x0, other arithmetic: 64.9 us -> none  [the longest x4 64.9 us: local(): nxt = 2.0 * now - prev + coef * laplace(extended)]
    ppermute x8 -> x12, waiting for transfers between devices: 43.1 us -> 6.8 us  [the longest x8 6.78 us: swap_faces(): return [lax.ppermute(half, 'space', across) for half in halves]]
    ppermute x8 -> x12, starting transfers between devices: 25.3 us -> 50.6 us  [the longest x8 42.9 us: swap_faces(): return [lax.ppermute(half, 'space', across) for half in halves]]
    pallas_call x0 -> x15, Pallas kernels: none -> 21.1 us  [call(): pl.pallas_call(kernel, out_shape=[jax.ShapeDtypeStruct(shape, F32) for sh...]
    all_to_all x4 -> x1, starting transfers between devices: 21.3 us -> 4.89 us  [local(): lax.all_to_all(zone, 'group', split_axis=0, concat_axis=0, tiled=True)]
    slice x6 -> x0, local copies, waits for them, and re-layouts: 5.02 us -> none  [the longest x4 3.72 us: padded_2(): lax.slice_in_dim(block, 0, width, axis=dim)]
    all_to_all x4 -> x1, waiting for transfers between devices: 12.8 us -> 9.45 us  [local(): lax.all_to_all(zone, 'group', split_axis=0, concat_axis=0, tiled=True)]
    reduce_prod x4 -> x0, other arithmetic: 1.98 us -> none  [product_groups(): return jnp.prod(received, axis=0)]
  transfers between devices with their start and end apart: 12 -> 13, of which waited for: 7 -> 3; matrix products, arithmetic and copies ran while one was open for 22% -> 1% of each run, Pallas kernels for 0% -> 18%
where the time goes in v1:
time: 99.1 us; the launch traced here: 98.5 us
  starting transfers between devices  55.5 us (56%)
  Pallas kernels  21.1 us (21%)
  waiting for transfers between devices  16.3 us (16%)
  local copies, waits for them, and re-layouts  4.65 us (5%)
    ppermute x8, starting transfers between devices, swap_faces(): return [lax.ppermute(half, 'space', across) for half in halves]  42.9 us
    pallas_call x15, Pallas kernels, call(): pl.pallas_call(kernel, out_shape=[jax.ShapeDtypeStruct(shape, F32) for sh...  21.1 us
    all_to_all x1, waiting for transfers between devices, local(): lax.all_to_all(zone, 'group', split_axis=0, concat_axis=0, tiled=True)  9.45 us
    ppermute x8, waiting for transfers between devices, swap_faces(): return [lax.ppermute(half, 'space', across) for half in halves]  6.78 us
    ppermute x3, starting transfers between devices, local(): halo = lax.ppermute(full, 'space', inside)  5.76 us
    all_to_all x1, starting transfers between devices, local(): lax.all_to_all(zone, 'group', split_axis=0, concat_axis=0, tiled=True)  4.89 us
  transfers between devices with their start and end apart: 13, of which 3 were waited for; matrix products, arithmetic and copies ran while one was open for 1% of the time, Pallas kernels for 18%

profile of v1, /device:TPU:32, one launch (start us, length us, event | category | flops | bytes accessed | tf_op | source)
XLA Modules:
  0.0 98.5 jit_solution(11170883313036008670)
XLA Ops:
  0.7 1.9 %dynamic-slice_bitcast_fusion.1 = (f32[4,64,256]{2,1,0:T(8,128)S(1)}, f32[4,64,256]{2,1,0:T(8,128)}) fusion(f32[1,8,128,256]{3,2,1,0:T(8,128)} %param.7, s32[]{:T(128)S(6)} %select_n.7), kind=kLoop, calls=%fused_computation.1 | loop fusion | bytes 1048580 | tf_op jit(solution)/shard_map/dynamic_slice | solution.py:288
  2.6 10.3 %collective-permute-start = (f32[4,64,256]{2,1,0:T(8,128)}, f32[4,64,256]{2,1,0:T(8,128)S(1)}, u32[]{:S(2)}, u32[]{:S(2)}) collective-permute-start(f32[4,64,256]{2,1,0:T(8,128)} %get-tuple-element.52), channel_id=1, source_target_pairs={{1,2},{3,4},{5,6},{7,8},{9,10},{11,12},{13,14},{15,16},{17,18},{19... | collective-permute-start | bytes 786440 | tf_op jit(solution)/shard_map/ppermute | solution.py:285
  12.8 1.9 %collective-permute-start.1 = (f32[4,64,256]{2,1,0:T(8,128)S(1)}, f32[4,64,256]{2,1,0:T(8,128)S(1)}, u32[]{:S(2)}, u32[]{:S(2)}) collective-permute-start(f32[4,64,256]{2,1,0:T(8,128)S(1)} %get-tuple-element.51), channel_id=1, source_target_pairs={{1,2},{3,4},{5,6},{7,8},{9,10},{11,12},{13,14},{15,16},{17,18},{19... | collective-permute-start | bytes 786440 | tf_op jit(solution)/shard_map/ppermute | solution.py:285
  14.8 0.8 dynamic-slice_bitcast_fusion
  15.6 1.9 %collective-permute-start.2 = (f32[4,128,256]{2,1,0:T(8,128)}, f32[4,128,256]{2,1,0:T(8,128)S(1)}, u32[]{:S(2)}, u32[]{:S(2)}) collective-permute-start(f32[4,128,256]{2,1,0:T(8,128)} %dynamic-slice_bitcast_fusion), channel_id=1, source_target_pairs={{0,1},{1,0},{2,3},{3,2},{4,5},{5,4},{6,7},{7,6},{8,9},{9,8},{10,11... | collective-permute-start | bytes 1572872 | tf_op jit(solution)/shard_map/ppermute | solution.py:290
  17.6 0.7 copy-done.5
  18.3 1.2 %copy-done.2 = s32[8,128,256]{2,1,0:T(8,128)S(1)} copy-done((s32[8,128,256]{2,1,0:T(8,128)S(1)}, s32[8,128,256]{2,1,0:T(8,128)}, u32[]{:S(2)}) %copy-start.2) | copy-done | bytes 1048600
  19.5 2.9 %shard_map.85 = (f32[8,128,256]{2,1,0:T(8,128)S(1)}, f32[4,128,256]{2,1,0:T(8,128)S(1)}, f32[4,128,256]{2,1,0:T(8,128)S(1)}) custom-call(s32[2]{0:T(128)S(1)} %pad_add_fusion.place, f32[16]{0:T(128)S(1)} %copy-done.5, f32[8,128,256]{2,1,0:T(8,128)S(1)} %bitcast.12, f32[8,128,256]{2,1,0:T(8,128)S(1)} %bitcast.14, s32[8,128,256]{2,1,0:T(8,128)S(1)} %copy-done.2), custom_call_target="tpu_custom_call" | custom-call | flops 1 | bytes 1 | tf_op jit(solution)/shard_map/pallas_call | solution.py:49
  22.5 0.7 shard_map.86.refs_1_.n1.refs_0_
  23.1 7.9 %collective-permute-start.3 = (f32[4,64,256]{2,1,0:T(8,128)S(1)}, f32[4,64,256]{2,1,0:T(8,128)S(1)}, u32[]{:S(2)}, u32[]{:S(2)}) collective-permute-start(f32[4,64,256]{2,1,0:T(8,128)S(1)} %shard_map.86.refs_1_.n1.refs_0_), channel_id=1, source_target_pairs={{1,2},{3,4},{5,6},{7,8},{9,10},{11,12},{13,14},{15,16},{17,18},{19... | collective-permute-start | bytes 786440 | tf_op jit(solution)/shard_map/ppermute | solution.py:285
  31.0 0.7 shard_map.87
  31.7 1.9 %collective-permute-start.4 = (f32[4,64,256]{2,1,0:T(8,128)S(1)}, f32[4,64,256]{2,1,0:T(8,128)S(1)}, u32[]{:S(2)}, u32[]{:S(2)}) collective-permute-start(f32[4,64,256]{2,1,0:T(8,128)S(1)} %get-tuple-element.30.n2.refs_1_), channel_id=1, source_target_pairs={{1,2},{3,4},{5,6},{7,8},{9,10},{11,12},{13,14},{15,16},{17,18},{19... | collective-permute-start | bytes 786440 | tf_op jit(solution)/shard_map/ppermute | solution.py:285
  33.6 2.4 %shard_map.88 = (f32[4,128,256]{2,1,0:T(8,128)S(1)}, f32[4,128,256]{2,1,0:T(8,128)S(1)}, f32[4,128,256]{2,1,0:T(8,128)S(1)}, f32[8,1,8,8,128]{4,3,2,1,0:T(8,128)S(1)}) custom-call(s32[2]{0:T(128)S(1)} %pad_add_fusion.place, s32[2]{0:T(128)S(1)} %copy-done.4, f32[4,64,256]{2,1,0:T(8,128)S(1)} %shard_map.86.refs_1_.n1.refs_0_, ...), custom_call_target="tpu_custom_call" | custom-call | flops 1 | bytes 1 | tf_op jit(solution)/shard_map/pallas_call | solution.py:49
  36.0 1.9 %collective-permute-start.5 = (f32[4,128,256]{2,1,0:T(8,128)S(1)}, f32[4,128,256]{2,1,0:T(8,128)S(1)}, u32[]{:S(2)}, u32[]{:S(2)}) collective-permute-start(f32[4,128,256]{2,1,0:T(8,128)S(1)} %get-tuple-element.36.refs_2_), channel_id=1, source_target_pairs={{0,1},{1,0},{2,3},{3,2},{4,5},{5,4},{6,7},{7,6},{8,9},{9,8},{10,11... | collective-permute-start | bytes 1572872 | tf_op jit(solution)/shard_map/ppermute | solution.py:332
  38.0 0.6 shard_map.89.refs_1_.n1.refs_0_
  38.6 7.9 %collective-permute-start.6 = (f32[4,64,256]{2,1,0:T(8,128)S(1)}, f32[4,64,256]{2,1,0:T(8,128)S(1)}, u32[]{:S(2)}, u32[]{:S(2)}) collective-permute-start(f32[4,64,256]{2,1,0:T(8,128)S(1)} %shard_map.89.refs_1_.n1.refs_0_), channel_id=1, source_target_pairs={{1,2},{3,4},{5,6},{7,8},{9,10},{11,12},{13,14},{15,16},{17,18},{19... | collective-permute-start | bytes 786440 | tf_op jit(solution)/shard_map/ppermute | solution.py:285
  46.5 0.6 shard_map.90
  47.1 3.3 %collective-permute-start.7 = (f32[4,64,256]{2,1,0:T(8,128)S(1)}, f32[4,64,256]{2,1,0:T(8,128)S(1)}, u32[]{:S(2)}, u32[]{:S(2)}) collective-permute-start(f32[4,64,256]{2,1,0:T(8,128)S(1)} %get-tuple-element.34.n2.refs_1_), channel_id=1, source_target_pairs={{1,2},{3,4},{5,6},{7,8},{9,10},{11,12},{13,14},{15,16},{17,18},{19... | collective-permute-start | bytes 786440 | tf_op jit(solution)/shard_map/ppermute | solution.py:285
  50.4 2.4 %shard_map.91 = (f32[4,128,256]{2,1,0:T(8,128)S(1)}, f32[4,128,256]{2,1,0:T(8,128)S(1)}, f32[4,128,256]{2,1,0:T(8,128)S(1)}, f32[8,2,8,8,128]{4,3,2,1,0:T(8,128)S(1)}) custom-call(s32[2]{0:T(128)S(1)} %pad_add_fusion.place, s32[2]{0:T(128)S(1)} %copy-done.4, f32[4,64,256]{2,1,0:T(8,128)S(1)} %shard_map.89.refs_1_.n1.refs_0_, ...), custom_call_target="tpu_custom_call" | custom-call | flops 1 | bytes 1 | tf_op jit(solution)/shard_map/pallas_call | solution.py:49
  52.8 1.9 %collective-permute-start.8 = (f32[4,128,256]{2,1,0:T(8,128)S(1)}, f32[4,128,256]{2,1,0:T(8,128)S(1)}, u32[]{:S(2)}, u32[]{:S(2)}) collective-permute-start(f32[4,128,256]{2,1,0:T(8,128)S(1)} %get-tuple-element.42.refs_2_), channel_id=1, source_target_pairs={{0,1},{1,0},{2,3},{3,2},{4,5},{5,4},{6,7},{7,6},{8,9},{9,8},{10,11... | collective-permute-start | bytes 1572872 | tf_op jit(solution)/shard_map/ppermute | solution.py:332
  54.7 0.6 shard_map.92.refs_1_.n1
  55.4 6.5 %collective-permute-start.9 = (f32[4,64,256]{2,1,0:T(8,128)S(1)}, f32[4,64,256]{2,1,0:T(8,128)S(1)}, u32[]{:S(2)}, u32[]{:S(2)}) collective-permute-start(f32[4,64,256]{2,1,0:T(8,128)S(1)} %shard_map.92.refs_1_.n1), channel_id=1, source_target_pairs={{1,2},{3,4},{5,6},{7,8},{9,10},{11,12},{13,14},{15,16},{17,18},{19... | collective-permute-start | bytes 786440 | tf_op jit(solution)/shard_map/ppermute | solution.py:285
  62.7 3.3 %collective-permute-start.10 = (f32[4,64,256]{2,1,0:T(8,128)S(1)}, f32[4,64,256]{2,1,0:T(8,128)S(1)}, u32[]{:S(2)}, u32[]{:S(2)}) collective-permute-start(f32[4,64,256]{2,1,0:T(8,128)S(1)} %get-tuple-element.40.n2), channel_id=1, source_target_pairs={{1,2},{3,4},{5,6},{7,8},{9,10},{11,12},{13,14},{15,16},{17,18},{19... | collective-permute-start | bytes 786440 | tf_op jit(solution)/shard_map/ppermute | solution.py:285
  66.0 2.4 %shard_map.94 = (f32[4,128,256]{2,1,0:T(8,128)S(1)}, f32[4,128,256]{2,1,0:T(8,128)S(1)}, f32[4,128,256]{2,1,0:T(8,128)S(1)}, f32[8,3,8,8,128]{4,3,2,1,0:T(8,128)S(1)}) custom-call(s32[2]{0:T(128)S(1)} %pad_add_fusion.place, s32[2]{0:T(128)S(1)} %copy-done.4, f32[4,64,256]{2,1,0:T(8,128)S(1)} %shard_map.92.refs_1_.n1, ...), custom_call_target="tpu_custom_call" | custom-call | flops 1 | bytes 1 | tf_op jit(solution)/shard_map/pallas_call | solution.py:49
  68.4 1.9 %collective-permute-start.11 = (f32[4,128,256]{2,1,0:T(8,128)S(1)}, f32[4,128,256]{2,1,0:T(8,128)S(1)}, u32[]{:S(2)}, u32[]{:S(2)}) collective-permute-start(f32[4,128,256]{2,1,0:T(8,128)S(1)} %get-tuple-element.44.na), channel_id=1, source_target_pairs={{0,1},{1,0},{2,3},{3,2},{4,5},{5,4},{6,7},{7,6},{8,9},{9,8},{10,11... | collective-permute-start | bytes 1572872 | tf_op jit(solution)/shard_map/ppermute | solution.py:332
  71.0 6.6 %collective-permute-done.10.halo = f32[4,64,256]{2,1,0:T(8,128)S(1)} collective-permute-done((f32[4,64,256]{2,1,0:T(8,128)S(1)}, f32[4,64,256]{2,1,0:T(8,128)S(1)}, u32[]{:S(2)}, u32[]{:S(2)}) %collective-permute-start.10) | collective-permute-done | bytes 262176 | tf_op jit(solution)/shard_map/ppermute | solution.py:285
  77.6 2.1 %shard_map.97 = (f32[4,64,256]{2,1,0:T(8,128)S(1)}, f32[4,128,256]{2,1,0:T(8,128)S(1)}, f32[8,4,8,8,128]{4,3,2,1,0:T(8,128)}) custom-call(s32[2]{0:T(128)S(1)} %copy-done.4, f32[4,128,256]{2,1,0:T(8,128)S(1)} %get-tuple-element.45.base, f32[8,128,256]{2,1,0:T(8,128)S(1)} %get-tuple-element.28.coef.refs_1_.refs_3_, ...), custom_call_target="tpu_custom_call" | custom-call | flops 1 | bytes 1 | tf_op jit(solution)/shard_map/pallas_call | solution.py:49
  79.7 4.9 %all-to-all-start = ((f32[8,4,8,8,128]{4,3,2,1,0:T(8,128)}), f32[8,4,8,8,128]{4,3,2,1,0:T(8,128)S(1)}, u32[]{:S(2)}, u32[]{:S(2)}) async-start(f32[8,4,8,8,128]{4,3,2,1,0:T(8,128)} %get-tuple-element.50), calls=%async_computation | async-start | bytes 2097152 | tf_op jit(solution)/shard_map/all_to_all | solution.py:348
  84.6 1.6 %shard_map.95 = f32[8,128,256]{2,1,0:T(8,128)} custom-call(s32[2]{0:T(128)S(1)} %pad_add_fusion.place, f32[4,64,256]{2,1,0:T(8,128)S(1)} %shard_map.92.refs_1_.n1, f32[4,64,256]{2,1,0:T(8,128)S(1)} %get-tuple-element.40.n2, f32[4,128,256]{2,1,0:T(8,128)S(1)} %get-tuple-element.44.na), custom_call_target="tpu_custom_call" | custom-call | flops 1 | bytes 1 | tf_op jit(solution)/shard_map/pallas_call | solution.py:49
  86.2 1.6 %shard_map.98 = f32[8,128,256]{2,1,0:T(8,128)} custom-call(s32[2]{0:T(128)S(1)} %pad_add_fusion.place, f32[4,64,256]{2,1,0:T(8,128)S(1)} %shard_map.96.n1, f32[4,64,256]{2,1,0:T(8,128)S(1)} %get-tuple-element.48.n2, f32[4,128,256]{2,1,0:T(8,128)S(1)} %get-tuple-element.49.na), custom_call_target="tpu_custom_call" | custom-call | flops 1 | bytes 1 | tf_op jit(solution)/shard_map/pallas_call | solution.py:49
  87.8 9.5 %all-to-all-done.received = f32[8,4,8,8,128]{4,3,2,1,0:T(8,128)S(1)} async-done(((f32[8,4,8,8,128]{4,3,2,1,0:T(8,128)}), f32[8,4,8,8,128]{4,3,2,1,0:T(8,128)S(1)}, u32[]{:S(2)}, u32[]{:S(2)}) %all-to-all-start) | async-done | bytes 1048608 | tf_op jit(solution)/shard_map/all_to_all | solution.py:348
  97.3 1.2 %shard_map.99 = f32[8,8,128]{2,1,0:T(8,128)} custom-call(s32[2]{0:T(128)S(1)} %pad_add_fusion.place, f32[8,8,128]{2,1,0:T(8,128)S(1)} %copy-done.3, f32[8,4,8,8,128]{4,3,2,1,0:T(8,128)S(1)} %all-to-all-done.received), custom_call_target="tpu_custom_call" | custom-call | flops 1 | bytes 1 | tf_op jit(solution)/shard_map/pallas_call | solution.py:49
  (24 shorter events, 1.5 us)
Async XLA Ops:
  0.6 14.1 %copy-start = (f32[1,8,128,256]{3,2,1,0:T(8,128)S(1)}, f32[1,8,128,256]{3,2,1,0:T(8,128)}, u32[]{:S(2)}) copy-start(f32[1,8,128,256]{3,2,1,0:T(8,128)} %param.7) | copy-start | bytes 3145732
  0.7 17.0 %copy-start.1 = (f32[1,8,128,256]{3,2,1,0:T(8,128)S(1)}, f32[1,8,128,256]{3,2,1,0:T(8,128)}, u32[]{:S(2)}) copy-start(f32[1,8,128,256]{3,2,1,0:T(8,128)} %param.6) | copy-start | bytes 3145732
  2.6 19.9 %collective-permute-start = (f32[4,64,256]{2,1,0:T(8,128)}, f32[4,64,256]{2,1,0:T(8,128)S(1)}, u32[]{:S(2)}, u32[]{:S(2)}) collective-permute-start(f32[4,64,256]{2,1,0:T(8,128)} %get-tuple-element.52), channel_id=1, source_target_pairs={{1,2},{3,4},{5,6},{7,8},{9,10},{11,12},{13,14},{15,16},{17,18},{19... | collective-permute-start | bytes 786440 | tf_op jit(solution)/shard_map/ppermute | solution.py:285
  12.8 18.1 %collective-permute-start.1 = (f32[4,64,256]{2,1,0:T(8,128)S(1)}, f32[4,64,256]{2,1,0:T(8,128)S(1)}, u32[]{:S(2)}, u32[]{:S(2)}) collective-permute-start(f32[4,64,256]{2,1,0:T(8,128)S(1)} %get-tuple-element.51), channel_id=1, source_target_pairs={{1,2},{3,4},{5,6},{7,8},{9,10},{11,12},{13,14},{15,16},{17,18},{19... | collective-permute-start | bytes 786440 | tf_op jit(solution)/shard_map/ppermute | solution.py:285
  15.6 18.0 %collective-permute-start.2 = (f32[4,128,256]{2,1,0:T(8,128)}, f32[4,128,256]{2,1,0:T(8,128)S(1)}, u32[]{:S(2)}, u32[]{:S(2)}) collective-permute-start(f32[4,128,256]{2,1,0:T(8,128)} %dynamic-slice_bitcast_fusion), channel_id=1, source_target_pairs={{0,1},{1,0},{2,3},{3,2},{4,5},{5,4},{6,7},{7,6},{8,9},{9,8},{10,11... | collective-permute-start | bytes 1572872 | tf_op jit(solution)/shard_map/ppermute | solution.py:290
  17.6 0.7 copy-start.5
  18.3 1.2 %copy-start.2 = (s32[8,128,256]{2,1,0:T(8,128)S(1)}, s32[8,128,256]{2,1,0:T(8,128)}, u32[]{:S(2)}) copy-start(s32[8,128,256]{2,1,0:T(8,128)} %regions.1) | copy-start | bytes 3145732
  23.1 14.8 %collective-permute-start.3 = (f32[4,64,256]{2,1,0:T(8,128)S(1)}, f32[4,64,256]{2,1,0:T(8,128)S(1)}, u32[]{:S(2)}, u32[]{:S(2)}) collective-permute-start(f32[4,64,256]{2,1,0:T(8,128)S(1)} %shard_map.86.refs_1_.n1.refs_0_), channel_id=1, source_target_pairs={{1,2},{3,4},{5,6},{7,8},{9,10},{11,12},{13,14},{15,16},{17,18},{19... | collective-permute-start | bytes 786440 | tf_op jit(solution)/shard_map/ppermute | solution.py:285
  31.7 2.0 %copy-start.4 = (s32[2]{0:T(128)S(1)}, s32[2]{0:T(128)}, u32[]{:S(2)}) copy-start(s32[2]{0:T(128)} %box.7) | copy-start | bytes 28
  31.7 14.8 %collective-permute-start.4 = (f32[4,64,256]{2,1,0:T(8,128)S(1)}, f32[4,64,256]{2,1,0:T(8,128)S(1)}, u32[]{:S(2)}, u32[]{:S(2)}) collective-permute-start(f32[4,64,256]{2,1,0:T(8,128)S(1)} %get-tuple-element.30.n2.refs_1_), channel_id=1, source_target_pairs={{1,2},{3,4},{5,6},{7,8},{9,10},{11,12},{13,14},{15,16},{17,18},{19... | collective-permute-start | bytes 786440 | tf_op jit(solution)/shard_map/ppermute | solution.py:285
  36.0 14.4 %collective-permute-start.5 = (f32[4,128,256]{2,1,0:T(8,128)S(1)}, f32[4,128,256]{2,1,0:T(8,128)S(1)}, u32[]{:S(2)}, u32[]{:S(2)}) collective-permute-start(f32[4,128,256]{2,1,0:T(8,128)S(1)} %get-tuple-element.36.refs_2_), channel_id=1, source_target_pairs={{0,1},{1,0},{2,3},{3,2},{4,5},{5,4},{6,7},{7,6},{8,9},{9,8},{10,11... | collective-permute-start | bytes 1572872 | tf_op jit(solution)/shard_map/ppermute | solution.py:332
  38.6 16.1 %collective-permute-start.6 = (f32[4,64,256]{2,1,0:T(8,128)S(1)}, f32[4,64,256]{2,1,0:T(8,128)S(1)}, u32[]{:S(2)}, u32[]{:S(2)}) collective-permute-start(f32[4,64,256]{2,1,0:T(8,128)S(1)} %shard_map.89.refs_1_.n1.refs_0_), channel_id=1, source_target_pairs={{1,2},{3,4},{5,6},{7,8},{9,10},{11,12},{13,14},{15,16},{17,18},{19... | collective-permute-start | bytes 786440 | tf_op jit(solution)/shard_map/ppermute | solution.py:285
  47.1 14.9 %collective-permute-start.7 = (f32[4,64,256]{2,1,0:T(8,128)S(1)}, f32[4,64,256]{2,1,0:T(8,128)S(1)}, u32[]{:S(2)}, u32[]{:S(2)}) collective-permute-start(f32[4,64,256]{2,1,0:T(8,128)S(1)} %get-tuple-element.34.n2.refs_1_), channel_id=1, source_target_pairs={{1,2},{3,4},{5,6},{7,8},{9,10},{11,12},{13,14},{15,16},{17,18},{19... | collective-permute-start | bytes 786440 | tf_op jit(solution)/shard_map/ppermute | solution.py:285
  52.8 13.2 %collective-permute-start.8 = (f32[4,128,256]{2,1,0:T(8,128)S(1)}, f32[4,128,256]{2,1,0:T(8,128)S(1)}, u32[]{:S(2)}, u32[]{:S(2)}) collective-permute-start(f32[4,128,256]{2,1,0:T(8,128)S(1)} %get-tuple-element.42.refs_2_), channel_id=1, source_target_pairs={{0,1},{1,0},{2,3},{3,2},{4,5},{5,4},{6,7},{7,6},{8,9},{9,8},{10,11... | collective-permute-start | bytes 1572872 | tf_op jit(solution)/shard_map/ppermute | solution.py:332
  55.4 14.9 %collective-permute-start.9 = (f32[4,64,256]{2,1,0:T(8,128)S(1)}, f32[4,64,256]{2,1,0:T(8,128)S(1)}, u32[]{:S(2)}, u32[]{:S(2)}) collective-permute-start(f32[4,64,256]{2,1,0:T(8,128)S(1)} %shard_map.92.refs_1_.n1), channel_id=1, source_target_pairs={{1,2},{3,4},{5,6},{7,8},{9,10},{11,12},{13,14},{15,16},{17,18},{19... | collective-permute-start | bytes 786440 | tf_op jit(solution)/shard_map/ppermute | solution.py:285
  62.7 14.9 %collective-permute-start.10 = (f32[4,64,256]{2,1,0:T(8,128)S(1)}, f32[4,64,256]{2,1,0:T(8,128)S(1)}, u32[]{:S(2)}, u32[]{:S(2)}) collective-permute-start(f32[4,64,256]{2,1,0:T(8,128)S(1)} %get-tuple-element.40.n2), channel_id=1, source_target_pairs={{1,2},{3,4},{5,6},{7,8},{9,10},{11,12},{13,14},{15,16},{17,18},{19... | collective-permute-start | bytes 786440 | tf_op jit(solution)/shard_map/ppermute | solution.py:285
  68.4 9.2 %collective-permute-start.11 = (f32[4,128,256]{2,1,0:T(8,128)S(1)}, f32[4,128,256]{2,1,0:T(8,128)S(1)}, u32[]{:S(2)}, u32[]{:S(2)}) collective-permute-start(f32[4,128,256]{2,1,0:T(8,128)S(1)} %get-tuple-element.44.na), channel_id=1, source_target_pairs={{0,1},{1,0},{2,3},{3,2},{4,5},{5,4},{6,7},{7,6},{8,9},{9,8},{10,11... | collective-permute-start | bytes 1572872 | tf_op jit(solution)/shard_map/ppermute | solution.py:332
  79.7 17.6 %all-to-all-start = ((f32[8,4,8,8,128]{4,3,2,1,0:T(8,128)}), f32[8,4,8,8,128]{4,3,2,1,0:T(8,128)S(1)}, u32[]{:S(2)}, u32[]{:S(2)}) async-start(f32[8,4,8,8,128]{4,3,2,1,0:T(8,128)} %get-tuple-element.50), calls=%async_computation | async-start | bytes 2097152 | tf_op jit(solution)/shard_map/all_to_all | solution.py:348
  86.2 11.1 %copy-start.3 = (f32[8,8,128]{2,1,0:T(8,128)S(1)}, f32[8,8,128]{2,1,0:T(8,128)}, u32[]{:S(2)}) copy-start(f32[8,8,128]{2,1,0:T(8,128)} %image.1) | copy-start | bytes 98308

commit v2 on v1

--- a/solution.py
+++ b/solution.py
@@ -23,7 +23,6 @@
 BF16 = jnp.bfloat16
 
 VM = pl.BlockSpec(memory_space=pltpu.VMEM)
-SM = pl.BlockSpec(memory_space=pltpu.SMEM)
 ANY = pl.BlockSpec(memory_space=pl.ANY)
 
 
@@ -58,6 +57,10 @@
     )(*args)
 
 
+def flip_of():
+    return 7 * lax.rem(lax.axis_index("space"), 2)
+
+
 def thirds(x):
     high = x.astype(BF16)
     left = x - high.astype(F32)
@@ -79,11 +82,9 @@
 
 def advance(now, older, coef_of, cross, store_base, store_next):
     for half in range(HALVES):
-
-        @pl.loop(0, ROWS // 8)
-        def _(block):
-            inner = pl.ds(pl.multiple_of(block * 8, 8), 8)
-            outer = pl.ds(pl.multiple_of(half * ROWS + block * 8, 8), 8)
+        for block in range(ROWS // 8):
+            inner = pl.ds(block * 8, 8)
+            outer = pl.ds(half * ROWS + block * 8, 8)
             at = (inner, outer, half)
             values = [now(j, at) for j in range(PLANES)]
             for j in range(PLANES):
@@ -118,9 +119,13 @@
     return jnp.concatenate([first[j], second[j]], axis=0)
 
 
+def first_cell(box_ref):
+    return [jnp.max(box_ref[i]).astype(jnp.int32) for i in range(2)]
+
+
 def cut_zone(plane, box):
-    moved = pltpu.roll(plane, (NY - box[0]) % NY, 0)[:ZY]
-    return pltpu.roll(moved, (NZ - box[1]) % NZ, 1)[:, :ZZ]
+    moved = pltpu.roll(plane, (NZ - box[1]) % NZ, 1)[:, :ZZ]
+    return pltpu.roll(moved, (NY - box[0]) % NY, 0)[:ZY]
 
 
 def split_zone(plane, box):
@@ -134,12 +139,17 @@
     return put
 
 
-def first_kernel(place, table, now, prev, regions, coef, base, rest, cross, across_y, across_z):
-    flip = place[0]
+def first_kernel(
+    table_ref, now, prev, regions, coef, base, rest, cross, across_y, across_z, table, sem
+):
+    load = pltpu.make_async_copy(table_ref, table, sem)
+    load.start()
+    flip = flip_of()
     store_bands(across_y, across_z)
-    scaled = [table[i] * (1.0 / SCALE) for i in range(16)]
     for j in range(PLANES):
         cross[j] = cross_terms(now[j ^ flip], across_y[...], across_z[...])
+    load.wait()
+    scaled = [table[i] * (1.0 / SCALE) for i in range(16)]
 
     def coef_of(j, at):
         code = regions[j ^ flip, at[1], :]
@@ -162,23 +172,24 @@
     )
 
 
-def middle_kernel(first, place, box, n1, n2, partial, halo, *refs):
+def middle_kernel(first, box_ref, n1, n2, partial, halo, *refs):
     *refs, now, base, nxt, zones, cross, across_y, across_z = refs
+    box = first_cell(box_ref)
     if first:
         prev, coef = refs
-        older = from_natural(prev, place[0])
+        older = from_natural(prev, flip_of())
         earlier = ()
     else:
         p1, p2, pa, coef, *earlier = refs
         older = from_parts(p1, p2, pa)
     for zone in earlier:
         zones[:, : zone.shape[1]] = zone[...]
-    far_terms(coef, partial, halo, 3 - place[1] if first else 0, now)
+    far_terms(coef, partial, halo, 3 & ~flip_of() if first else 0, now)
     store_bands(across_y, across_z)
     for j in range(PLANES):
-        plane = whole_plane(n1, n2, now, j)
-        cross[j] = cross_terms(plane, across_y[...], across_z[...])
-        zones[:, zones.shape[1] - 1, j] = split_zone(plane, box)
+        cross[j] = cross_terms(whole_plane(n1, n2, now, j), across_y[...], across_z[...])
+    for j in range(PLANES):
+        zones[:, zones.shape[1] - 1, j] = split_zone(whole_plane(n1, n2, now, j), box)
     advance(
         from_parts(n1, n2, now),
         older,
@@ -190,10 +201,9 @@
 
 
 def face_terms(base, coef, halo, turn, half, put):
-    @pl.loop(0, ROWS // 8)
-    def _(block):
-        inner = pl.ds(pl.multiple_of(block * 8, 8), 8)
-        outer = pl.ds(pl.multiple_of(half * ROWS + block * 8, 8), 8)
+    for block in range(ROWS // 8):
+        inner = pl.ds(block * 8, 8)
+        outer = pl.ds(half * ROWS + block * 8, 8)
         beyond = [halo[k ^ turn, inner, :] for k in range(FACE)]
         for j in range(FACE):
             total = TAPS[j] * beyond[0]
@@ -202,9 +212,9 @@
             put(j, inner, base[j, outer, :] + coef[j, outer, :] * total)
 
 
-def face_kernel(half, first, place, base, coef, halo, *refs):
+def face_kernel(half, first, base, coef, halo, *refs):
     out = refs[2 if half else 0]
-    turn = 3 - place[1] if first else 0
+    turn = 3 & ~flip_of() if first else 0
 
     def put(j, inner, value):
         out[j, inner, :] = value
@@ -213,9 +223,8 @@
 
 
 def far_terms(coef, partial, halo, turn, out):
-    @pl.loop(0, NY // 8)
-    def _(block):
-        rows = pl.ds(pl.multiple_of(block * 8, 8), 8)
+    for block in range(NY // 8):
+        rows = pl.ds(block * 8, 8)
         beyond = [halo[(FACE - 1 - k) ^ turn, rows, :] for k in range(FACE)]
         for j in range(FACE):
             total = TAPS[j] * beyond[0]
@@ -225,7 +234,11 @@
             out[mine, rows, :] = partial[mine, rows, :] + coef[FACE + mine, rows, :] * total
 
 
-def last_kernel(box, base, coef, halo, n1, partial, far_halo, earlier, n2, now, zones):
+def last_kernel(
+    box_ref, base, coef, halo, n1, partial, far_halo, earlier, n2, now, zones
+):
+    box = first_cell(box_ref)
+
     def put(j, inner, value):
         n2[j, inner, :] = value
 
@@ -236,8 +249,8 @@
         zones[:, STEPS - 1, j] = split_zone(whole_plane(n1, n2, now, j), box)
 
 
-def gather_kernel(place, n1, n2, na, out, sems):
-    flip = place[0]
+def gather_kernel(n1, n2, na, out, sems):
+    flip = flip_of()
     copies = []
     for j in range(FACE):
         copies.append((n1.at[j], out.at[j ^ flip, pl.ds(0, ROWS)]))
@@ -253,9 +266,9 @@
         copy.wait()
 
 
-def image_kernel(place, image, received, out):
+def image_kernel(image, received, out):
     for j in range(PLANES):
-        at = j ^ place[0]
+        at = j ^ flip_of()
         total = image[at]
         for step in range(received.shape[1]):
             product = received[0, step, j]
@@ -269,7 +282,6 @@
     prev = pressure_prev[0]
     now = pressure_now[0]
     odd = lax.rem(lax.axis_index("space"), 2)
-    place = jnp.stack([7 * odd, 3 * odd]).astype(jnp.int32)
     count = lax.axis_size("space")
     inside = [(i, i ^ 1) for i in range(count)]
     across = [(i, i + 1) for i in range(1, count - 1, 2)]
@@ -279,6 +291,7 @@
     slab_shape = (PLANES, NY, NZ)
     zone_rows = (ZY // GROUPS, ZZ)
     slab = pltpu.VMEM(slab_shape, F32)
+    box = jnp.broadcast_to(box.astype(F32)[:, None, None], (2, 8, 128))
     work = [slab, pltpu.VMEM((NY, 3 * NY), BF16), pltpu.VMEM((3 * NZ, NZ), BF16)]
 
     def swap_faces(halves):
@@ -293,10 +306,10 @@
     coef, base, rest = call(
         first_kernel,
         [slab_shape] + [face_shape] * 2,
-        [SM, SM] + [VM] * 3,
+        [ANY] + [VM] * 3,
         [VM] * 3,
-        (place, speed_table, now, prev, regions),
-        scratch=work,
+        (speed_table, now, prev, regions),
+        scratch=work + [pltpu.SMEM(speed_table.shape, F32), pltpu.SemaphoreType.DMA(())],
     )
     older = [now]
     zones = ()
@@ -304,26 +317,26 @@
         n1 = call(
             functools.partial(face_kernel, 0, step == 0),
             [half_shape],
-            [SM] + [VM] * 3,
+            [VM] * 3,
             [VM],
-            (place, base, coef, beyond[0]),
+            (base, coef, beyond[0]),
         )[0]
         n2, rest = call(
             functools.partial(face_kernel, 1, step == 0),
             [half_shape, face_shape],
-            [SM] + [VM] * 3 + [ANY] * 2,
+            [VM] * 3 + [ANY] * 2,
             [VM, ANY],
-            (place, base, coef, beyond[1], rest, n1),
+            (base, coef, beyond[1], rest, n1),
             cost=COST[1],
-            aliases={4: 1},
+            aliases={3: 1},
         )
         beyond = swap_faces([n1, n2])
         full, base, rest, zone = call(
             functools.partial(middle_kernel, step == 0),
             [face_shape] * 3 + [(GROUPS, step + 1, PLANES) + zone_rows],
-            [SM, SM] + [VM] * (5 + len(older) + len(zones)),
+            [VM] * (6 + len(older) + len(zones)),
             [VM] * 4,
-            (place, box, n1, n2, rest, halo, *older, coef, *zones),
+            (box, n1, n2, rest, halo, *older, coef, *zones),
             cost=COST[0] if step < STEPS - 2 else COST[2],
             scratch=work,
         )
@@ -333,15 +346,15 @@
     n1 = call(
         functools.partial(face_kernel, 0, False),
         [half_shape],
-        [SM] + [VM] * 3,
+        [VM] * 3,
         [VM],
-        (place, base, coef, beyond[0]),
+        (base, coef, beyond[0]),
         cost=COST[3],
     )[0]
     n2, full, zone = call(
         last_kernel,
         [half_shape, face_shape, (GROUPS, STEPS, PLANES) + zone_rows],
-        [SM] + [VM] * 7,
+        [VM] * 8,
         [VM] * 3,
         (box, base, coef, beyond[1], n1, rest, halo, zone),
     )
@@ -351,16 +364,16 @@
         return call(
             gather_kernel,
             [slab_shape],
-            [SM] + [ANY] * 3,
+            [ANY] * 3,
             [ANY],
-            (place, *three),
+            three,
             scratch=[pltpu.SemaphoreType.DMA((12,))],
         )[0]
 
     out_prev = gather(older)
     out_now = gather((n1, n2, full))
     total = call(
-        image_kernel, [image.shape], [SM] + [VM] * 2, [VM], (place, image, received)
+        image_kernel, [image.shape], [VM] * 2, [VM], (image, received)
     )[0]
     return (out_prev[None], out_now[None], total)
 

time: 99.1 us -> 92.7 us (0.935)
  Pallas kernels: 21.1 us -> 11.6 us
  waiting for transfers between devices: 16.3 us -> 20.8 us
  local copies, waits for them, and re-layouts: 4.65 us -> 3.22 us
    pallas_call x15, Pallas kernels: 21.1 us -> 11.6 us  [call(): pl.pallas_call(kernel, out_shape=[jax.ShapeDtypeStruct(shape, F32) for sh...]
    ppermute x8, waiting for transfers between devices: 6.78 us -> 10.6 us  [swap_faces(): return [lax.ppermute(half, 'space', across) for half in halves]]
  transfers between devices with their start and end apart: 13 -> 13, of which waited for: 3 -> 6; matrix products, arithmetic and copies ran while one was open for 1% -> 0% of each run, Pallas kernels for 18% -> 10%
where the time goes in v2:
time: 92.7 us; the launch traced here: 92.2 us
  starting transfers between devices  55.6 us (60%)
  waiting for transfers between devices  20.8 us (22%)
  Pallas kernels  11.6 us (13%)
  local copies, waits for them, and re-layouts  3.22 us (3%)
  between operations  0.96 us (1%)
    ppermute x8, starting transfers between devices, swap_faces(): return [lax.ppermute(half, 'space', across) for half in halves]  43.1 us
    pallas_call x15, Pallas kernels, call(): pl.pallas_call(kernel, out_shape=[jax.ShapeDtypeStruct(shape, F32) for sh...  11.6 us
    ppermute x8, waiting for transfers between devices, swap_faces(): return [lax.ppermute(half, 'space', across) for half in halves]  10.6 us
    all_to_all x1, waiting for transfers between devices, local(): lax.all_to_all(zone, 'group', split_axis=0, concat_axis=0, tiled=True)  10.1 us
    ppermute x3, starting transfers between devices, local(): halo = lax.ppermute(full, 'space', inside)  5.76 us
    all_to_all x1, starting transfers between devices, local(): lax.all_to_all(zone, 'group', split_axis=0, concat_axis=0, tiled=True)  4.82 us
    ppermute x1, starting transfers between devices, local(): lax.ppermute(lax.dynamic_slice(now, (4 - 4 * odd, 0, 0), face_shape), 'sp...  1.92 us
    unnamed x12, local copies, waits for them, and re-layouts  1.89 us
  transfers between devices with their start and end apart: 13, of which 6 were waited for; matrix products, arithmetic and copies ran while one was open for 0% of the time, Pallas kernels for 10%

profile of v2, /device:TPU:32, one launch (start us, length us, event | category | flops | bytes accessed | tf_op | source)
XLA Modules:
  0.0 92.2 jit_solution(16963604723748882088)
XLA Ops:
  0.7 1.2 %dynamic-slice_bitcast_fusion.1 = (f32[4,64,256]{2,1,0:T(8,128)S(1)}, f32[4,64,256]{2,1,0:T(8,128)S(1)}) fusion(f32[1,8,128,256]{3,2,1,0:T(8,128)} %param.7, s32[]{:T(128)S(6)} %select_n.7), kind=kLoop, calls=%fused_computation.1 | loop fusion | bytes 1048580 | tf_op jit(solution)/shard_map/dynamic_slice | solution.py:301
  1.9 10.3 %collective-permute-start = (f32[4,64,256]{2,1,0:T(8,128)S(1)}, f32[4,64,256]{2,1,0:T(8,128)S(1)}, u32[]{:S(2)}, u32[]{:S(2)}) collective-permute-start(f32[4,64,256]{2,1,0:T(8,128)S(1)} %get-tuple-element.52), channel_id=1, source_target_pairs={{1,2},{3,4},{5,6},{7,8},{9,10},{11,12},{13,14},{15,16},{17,18},{19... | collective-permute-start | bytes 786440 | tf_op jit(solution)/shard_map/ppermute | solution.py:298
  12.2 1.9 %collective-permute-start.1 = (f32[4,64,256]{2,1,0:T(8,128)S(1)}, f32[4,64,256]{2,1,0:T(8,128)S(1)}, u32[]{:S(2)}, u32[]{:S(2)}) collective-permute-start(f32[4,64,256]{2,1,0:T(8,128)S(1)} %get-tuple-element.51), channel_id=1, source_target_pairs={{1,2},{3,4},{5,6},{7,8},{9,10},{11,12},{13,14},{15,16},{17,18},{19... | collective-permute-start | bytes 786440 | tf_op jit(solution)/shard_map/ppermute | solution.py:298
  14.2 1.9 %collective-permute-start.2 = (f32[4,128,256]{2,1,0:T(8,128)S(1)}, f32[4,128,256]{2,1,0:T(8,128)S(1)}, u32[]{:S(2)}, u32[]{:S(2)}) collective-permute-start(f32[4,128,256]{2,1,0:T(8,128)S(1)} %dynamic-slice_bitcast_fusion), channel_id=1, source_target_pairs={{0,1},{1,0},{2,3},{3,2},{4,5},{5,4},{6,7},{7,6},{8,9},{9,8},{10,11... | collective-permute-start | bytes 1572872 | tf_op jit(solution)/shard_map/ppermute | solution.py:303
  16.1 0.6 copy-done.4
  16.7 1.2 %copy-done.2 = s32[8,128,256]{2,1,0:T(8,128)S(1)} copy-done((s32[8,128,256]{2,1,0:T(8,128)S(1)}, s32[8,128,256]{2,1,0:T(8,128)}, u32[]{:S(2)}) %copy-start.2) | copy-done | bytes 1048600
  18.0 2.2 %shard_map.85 = (f32[8,128,256]{2,1,0:T(8,128)S(1)}, f32[4,128,256]{2,1,0:T(8,128)S(1)}, f32[4,128,256]{2,1,0:T(8,128)S(1)}) custom-call(f32[16]{0:T(128)S(1)} %copy-done.4, f32[8,128,256]{2,1,0:T(8,128)S(1)} %bitcast.10, f32[8,128,256]{2,1,0:T(8,128)S(1)} %bitcast.12, s32[8,128,256]{2,1,0:T(8,128)S(1)} %copy-done.2), custom_call_target="tpu_custom_call" | custom-call | flops 1 | bytes 1 | tf_op jit(solution)/shard_map/pallas_call | solution.py:48
  20.3 7.9 %collective-permute-start.3 = (f32[4,64,256]{2,1,0:T(8,128)S(1)}, f32[4,64,256]{2,1,0:T(8,128)S(1)}, u32[]{:S(2)}, u32[]{:S(2)}) collective-permute-start(f32[4,64,256]{2,1,0:T(8,128)S(1)} %shard_map.86.refs_1_.n1.refs_0_), channel_id=1, source_target_pairs={{1,2},{3,4},{5,6},{7,8},{9,10},{11,12},{13,14},{15,16},{17,18},{19... | collective-permute-start | bytes 786440 | tf_op jit(solution)/shard_map/ppermute | solution.py:298
  28.3 3.1 %collective-permute-start.4 = (f32[4,64,256]{2,1,0:T(8,128)S(1)}, f32[4,64,256]{2,1,0:T(8,128)S(1)}, u32[]{:S(2)}, u32[]{:S(2)}) collective-permute-start(f32[4,64,256]{2,1,0:T(8,128)S(1)} %get-tuple-element.30.n2.refs_1_), channel_id=1, source_target_pairs={{1,2},{3,4},{5,6},{7,8},{9,10},{11,12},{13,14},{15,16},{17,18},{19... | collective-permute-start | bytes 786440 | tf_op jit(solution)/shard_map/ppermute | solution.py:298
  31.4 0.1 broadcast_in_dim.12.box_ref
  31.4 1.5 %shard_map.88 = (f32[4,128,256]{2,1,0:T(8,128)S(1)}, f32[4,128,256]{2,1,0:T(8,128)S(1)}, f32[4,128,256]{2,1,0:T(8,128)S(1)}, f32[8,1,8,8,128]{4,3,2,1,0:T(8,128)S(1)}) custom-call(f32[2,8,128]{2,1,0:T(8,128)S(1)} %broadcast_in_dim.12.box_ref, f32[4,64,256]{2,1,0:T(8,128)S(1)} %shard_map.86.refs_1_.n1.refs_0_, ...), custom_call_target="tpu_custom_call" | custom-call | flops 1 | bytes 1 | tf_op jit(solution)/shard_map/pallas_call | solution.py:48
  32.9 1.9 %collective-permute-start.5 = (f32[4,128,256]{2,1,0:T(8,128)S(1)}, f32[4,128,256]{2,1,0:T(8,128)S(1)}, u32[]{:S(2)}, u32[]{:S(2)}) collective-permute-start(f32[4,128,256]{2,1,0:T(8,128)S(1)} %get-tuple-element.36.refs_2_), channel_id=1, source_target_pairs={{0,1},{1,0},{2,3},{3,2},{4,5},{5,4},{6,7},{7,6},{8,9},{9,8},{10,11... | collective-permute-start | bytes 1572872 | tf_op jit(solution)/shard_map/ppermute | solution.py:345
  34.9 0.1 collective-permute-done.3.halo
  35.1 6.6 %collective-permute-start.6 = (f32[4,64,256]{2,1,0:T(8,128)S(1)}, f32[4,64,256]{2,1,0:T(8,128)S(1)}, u32[]{:S(2)}, u32[]{:S(2)}) collective-permute-start(f32[4,64,256]{2,1,0:T(8,128)S(1)} %shard_map.89.refs_1_.n1.refs_0_), channel_id=1, source_target_pairs={{1,2},{3,4},{5,6},{7,8},{9,10},{11,12},{13,14},{15,16},{17,18},{19... | collective-permute-start | bytes 786440 | tf_op jit(solution)/shard_map/ppermute | solution.py:298
  41.7 1.3 %collective-permute-done.4.halo = f32[4,64,256]{2,1,0:T(8,128)S(1)} collective-permute-done((f32[4,64,256]{2,1,0:T(8,128)S(1)}, f32[4,64,256]{2,1,0:T(8,128)S(1)}, u32[]{:S(2)}, u32[]{:S(2)}) %collective-permute-start.4) | collective-permute-done | bytes 262176 | tf_op jit(solution)/shard_map/ppermute | solution.py:298
  43.0 4.0 %collective-permute-start.7 = (f32[4,64,256]{2,1,0:T(8,128)S(1)}, f32[4,64,256]{2,1,0:T(8,128)S(1)}, u32[]{:S(2)}, u32[]{:S(2)}) collective-permute-start(f32[4,64,256]{2,1,0:T(8,128)S(1)} %get-tuple-element.34.n2.refs_1_), channel_id=1, source_target_pairs={{1,2},{3,4},{5,6},{7,8},{9,10},{11,12},{13,14},{15,16},{17,18},{19... | collective-permute-start | bytes 786440 | tf_op jit(solution)/shard_map/ppermute | solution.py:298
  47.1 1.5 %shard_map.91 = (f32[4,128,256]{2,1,0:T(8,128)S(1)}, f32[4,128,256]{2,1,0:T(8,128)S(1)}, f32[4,128,256]{2,1,0:T(8,128)S(1)}, f32[8,2,8,8,128]{4,3,2,1,0:T(8,128)S(1)}) custom-call(f32[2,8,128]{2,1,0:T(8,128)S(1)} %broadcast_in_dim.12.box_ref, f32[4,64,256]{2,1,0:T(8,128)S(1)} %shard_map.89.refs_1_.n1.refs_0_, ...), custom_call_target="tpu_custom_call" | custom-call | flops 1 | bytes 1 | tf_op jit(solution)/shard_map/pallas_call | solution.py:48
  48.6 1.9 %collective-permute-start.8 = (f32[4,128,256]{2,1,0:T(8,128)S(1)}, f32[4,128,256]{2,1,0:T(8,128)S(1)}, u32[]{:S(2)}, u32[]{:S(2)}) collective-permute-start(f32[4,128,256]{2,1,0:T(8,128)S(1)} %get-tuple-element.42.refs_2_), channel_id=1, source_target_pairs={{0,1},{1,0},{2,3},{3,2},{4,5},{5,4},{6,7},{7,6},{8,9},{9,8},{10,11... | collective-permute-start | bytes 1572872 | tf_op jit(solution)/shard_map/ppermute | solution.py:345
  50.6 0.1 shard_map.92.refs_1_.n1
  50.6 5.8 %collective-permute-start.9 = (f32[4,64,256]{2,1,0:T(8,128)S(1)}, f32[4,64,256]{2,1,0:T(8,128)S(1)}, u32[]{:S(2)}, u32[]{:S(2)}) collective-permute-start(f32[4,64,256]{2,1,0:T(8,128)S(1)} %shard_map.92.refs_1_.n1), channel_id=1, source_target_pairs={{1,2},{3,4},{5,6},{7,8},{9,10},{11,12},{13,14},{15,16},{17,18},{19... | collective-permute-start | bytes 786440 | tf_op jit(solution)/shard_map/ppermute | solution.py:298
  56.4 1.6 %collective-permute-done.7.halo = f32[4,64,256]{2,1,0:T(8,128)S(1)} collective-permute-done((f32[4,64,256]{2,1,0:T(8,128)S(1)}, f32[4,64,256]{2,1,0:T(8,128)S(1)}, u32[]{:S(2)}, u32[]{:S(2)}) %collective-permute-start.7) | collective-permute-done | bytes 262176 | tf_op jit(solution)/shard_map/ppermute | solution.py:298
  58.0 3.6 %collective-permute-start.10 = (f32[4,64,256]{2,1,0:T(8,128)S(1)}, f32[4,64,256]{2,1,0:T(8,128)S(1)}, u32[]{:S(2)}, u32[]{:S(2)}) collective-permute-start(f32[4,64,256]{2,1,0:T(8,128)S(1)} %get-tuple-element.40.n2), channel_id=1, source_target_pairs={{1,2},{3,4},{5,6},{7,8},{9,10},{11,12},{13,14},{15,16},{17,18},{19... | collective-permute-start | bytes 786440 | tf_op jit(solution)/shard_map/ppermute | solution.py:298
  61.6 1.6 %shard_map.94 = (f32[4,128,256]{2,1,0:T(8,128)S(1)}, f32[4,128,256]{2,1,0:T(8,128)S(1)}, f32[4,128,256]{2,1,0:T(8,128)S(1)}, f32[8,3,8,8,128]{4,3,2,1,0:T(8,128)S(1)}) custom-call(f32[2,8,128]{2,1,0:T(8,128)S(1)} %broadcast_in_dim.12.box_ref, f32[4,64,256]{2,1,0:T(8,128)S(1)} %shard_map.92.refs_1_.n1, f32[4,64,256]{2,1,0:T(8,128)S(1)} %get-tuple-element.40.n2, ...), custom_call_target="tpu_custom_call" | custom-call | flops 1 | bytes 1 | tf_op jit(solution)/shard_map/pallas_call | solution.py:48
  63.2 1.9 %collective-permute-start.11 = (f32[4,128,256]{2,1,0:T(8,128)S(1)}, f32[4,128,256]{2,1,0:T(8,128)S(1)}, u32[]{:S(2)}, u32[]{:S(2)}) collective-permute-start(f32[4,128,256]{2,1,0:T(8,128)S(1)} %get-tuple-element.44.na), channel_id=1, source_target_pairs={{0,1},{1,0},{2,3},{3,2},{4,5},{5,4},{6,7},{7,6},{8,9},{9,8},{10,11... | collective-permute-start | bytes 1572872 | tf_op jit(solution)/shard_map/ppermute | solution.py:345
  65.1 0.5 collective-permute-done.9.halo
  65.7 7.1 %collective-permute-done.10.halo = f32[4,64,256]{2,1,0:T(8,128)S(1)} collective-permute-done((f32[4,64,256]{2,1,0:T(8,128)S(1)}, f32[4,64,256]{2,1,0:T(8,128)S(1)}, u32[]{:S(2)}, u32[]{:S(2)}) %collective-permute-start.10) | collective-permute-done | bytes 262176 | tf_op jit(solution)/shard_map/ppermute | solution.py:298
  72.8 1.5 %shard_map.97 = (f32[4,64,256]{2,1,0:T(8,128)S(1)}, f32[4,128,256]{2,1,0:T(8,128)S(1)}, f32[8,4,8,8,128]{4,3,2,1,0:T(8,128)}) custom-call(f32[2,8,128]{2,1,0:T(8,128)S(1)} %broadcast_in_dim.12.box_ref, f32[4,128,256]{2,1,0:T(8,128)S(1)} %get-tuple-element.45.base, f32[8,128,256]{2,1,0:T(8,128)S(1)} %get-tuple-element.28.coef.refs_1_.refs_3_, ...), custom_call_target="tpu_custom_call" | custom-call | flops 1 | bytes 1 | tf_op jit(solution)/shard_map/pallas_call | solution.py:48
  74.4 4.8 %all-to-all-start = ((f32[8,4,8,8,128]{4,3,2,1,0:T(8,128)}), f32[8,4,8,8,128]{4,3,2,1,0:T(8,128)S(1)}, u32[]{:S(2)}, u32[]{:S(2)}) async-start(f32[8,4,8,8,128]{4,3,2,1,0:T(8,128)} %get-tuple-element.50), calls=%async_computation | async-start | bytes 2097152 | tf_op jit(solution)/shard_map/all_to_all | solution.py:361
  79.2 1.1 %shard_map.95 = f32[8,128,256]{2,1,0:T(8,128)} custom-call(f32[4,64,256]{2,1,0:T(8,128)S(1)} %shard_map.92.refs_1_.n1, f32[4,64,256]{2,1,0:T(8,128)S(1)} %get-tuple-element.40.n2, f32[4,128,256]{2,1,0:T(8,128)S(1)} %get-tuple-element.44.na), custom_call_target="tpu_custom_call" | custom-call | flops 1 | bytes 1 | tf_op jit(solution)/shard_map/pallas_call | solution.py:48
  80.3 1.1 %shard_map.98 = f32[8,128,256]{2,1,0:T(8,128)} custom-call(f32[4,64,256]{2,1,0:T(8,128)S(1)} %shard_map.96.n1, f32[4,64,256]{2,1,0:T(8,128)S(1)} %get-tuple-element.48.n2, f32[4,128,256]{2,1,0:T(8,128)S(1)} %get-tuple-element.49.na), custom_call_target="tpu_custom_call" | custom-call | flops 1 | bytes 1 | tf_op jit(solution)/shard_map/pallas_call | solution.py:48
  81.4 10.1 %all-to-all-done.received = f32[8,4,8,8,128]{4,3,2,1,0:T(8,128)S(1)} async-done(((f32[8,4,8,8,128]{4,3,2,1,0:T(8,128)}), f32[8,4,8,8,128]{4,3,2,1,0:T(8,128)S(1)}, u32[]{:S(2)}, u32[]{:S(2)}) %all-to-all-start) | async-done | bytes 1048608 | tf_op jit(solution)/shard_map/all_to_all | solution.py:361
  91.5 0.7 shard_map.99
  (25 shorter events, 0.5 us)
Async XLA Ops:
  0.6 13.5 %copy-start = (f32[1,8,128,256]{3,2,1,0:T(8,128)S(1)}, f32[1,8,128,256]{3,2,1,0:T(8,128)}, u32[]{:S(2)}) copy-start(f32[1,8,128,256]{3,2,1,0:T(8,128)} %param.7) | copy-start | bytes 3145732
  0.6 15.4 %copy-start.1 = (f32[1,8,128,256]{3,2,1,0:T(8,128)S(1)}, f32[1,8,128,256]{3,2,1,0:T(8,128)}, u32[]{:S(2)}) copy-start(f32[1,8,128,256]{3,2,1,0:T(8,128)} %param.6) | copy-start | bytes 3145732
  1.9 18.3 %collective-permute-start = (f32[4,64,256]{2,1,0:T(8,128)S(1)}, f32[4,64,256]{2,1,0:T(8,128)S(1)}, u32[]{:S(2)}, u32[]{:S(2)}) collective-permute-start(f32[4,64,256]{2,1,0:T(8,128)S(1)} %get-tuple-element.52), channel_id=1, source_target_pairs={{1,2},{3,4},{5,6},{7,8},{9,10},{11,12},{13,14},{15,16},{17,18},{19... | collective-permute-start | bytes 786440 | tf_op jit(solution)/shard_map/ppermute | solution.py:298
  12.2 16.0 %collective-permute-start.1 = (f32[4,64,256]{2,1,0:T(8,128)S(1)}, f32[4,64,256]{2,1,0:T(8,128)S(1)}, u32[]{:S(2)}, u32[]{:S(2)}) collective-permute-start(f32[4,64,256]{2,1,0:T(8,128)S(1)} %get-tuple-element.51), channel_id=1, source_target_pairs={{1,2},{3,4},{5,6},{7,8},{9,10},{11,12},{13,14},{15,16},{17,18},{19... | collective-permute-start | bytes 786440 | tf_op jit(solution)/shard_map/ppermute | solution.py:298
  14.2 17.2 %collective-permute-start.2 = (f32[4,128,256]{2,1,0:T(8,128)S(1)}, f32[4,128,256]{2,1,0:T(8,128)S(1)}, u32[]{:S(2)}, u32[]{:S(2)}) collective-permute-start(f32[4,128,256]{2,1,0:T(8,128)S(1)} %dynamic-slice_bitcast_fusion), channel_id=1, source_target_pairs={{0,1},{1,0},{2,3},{3,2},{4,5},{5,4},{6,7},{7,6},{8,9},{9,8},{10,11... | collective-permute-start | bytes 1572872 | tf_op jit(solution)/shard_map/ppermute | solution.py:303
  16.1 0.7 copy-start.4
  16.7 1.2 %copy-start.2 = (s32[8,128,256]{2,1,0:T(8,128)S(1)}, s32[8,128,256]{2,1,0:T(8,128)}, u32[]{:S(2)}) copy-start(s32[8,128,256]{2,1,0:T(8,128)} %regions.1) | copy-start | bytes 3145732
  20.3 14.7 %collective-permute-start.3 = (f32[4,64,256]{2,1,0:T(8,128)S(1)}, f32[4,64,256]{2,1,0:T(8,128)S(1)}, u32[]{:S(2)}, u32[]{:S(2)}) collective-permute-start(f32[4,64,256]{2,1,0:T(8,128)S(1)} %shard_map.86.refs_1_.n1.refs_0_), channel_id=1, source_target_pairs={{1,2},{3,4},{5,6},{7,8},{9,10},{11,12},{13,14},{15,16},{17,18},{19... | collective-permute-start | bytes 786440 | tf_op jit(solution)/shard_map/ppermute | solution.py:298
  28.2 3.1 %copy-start.5 = (s32[2]{0:T(128)S(1)}, s32[2]{0:T(128)}, u32[]{:S(2)}) copy-start(s32[2]{0:T(128)} %param.11) | copy-start | bytes 28
  28.3 14.7 %collective-permute-start.4 = (f32[4,64,256]{2,1,0:T(8,128)S(1)}, f32[4,64,256]{2,1,0:T(8,128)S(1)}, u32[]{:S(2)}, u32[]{:S(2)}) collective-permute-start(f32[4,64,256]{2,1,0:T(8,128)S(1)} %get-tuple-element.30.n2.refs_1_), channel_id=1, source_target_pairs={{1,2},{3,4},{5,6},{7,8},{9,10},{11,12},{13,14},{15,16},{17,18},{19... | collective-permute-start | bytes 786440 | tf_op jit(solution)/shard_map/ppermute | solution.py:298
  32.9 14.1 %collective-permute-start.5 = (f32[4,128,256]{2,1,0:T(8,128)S(1)}, f32[4,128,256]{2,1,0:T(8,128)S(1)}, u32[]{:S(2)}, u32[]{:S(2)}) collective-permute-start(f32[4,128,256]{2,1,0:T(8,128)S(1)} %get-tuple-element.36.refs_2_), channel_id=1, source_target_pairs={{0,1},{1,0},{2,3},{3,2},{4,5},{5,4},{6,7},{7,6},{8,9},{9,8},{10,11... | collective-permute-start | bytes 1572872 | tf_op jit(solution)/shard_map/ppermute | solution.py:345
  35.1 15.5 %collective-permute-start.6 = (f32[4,64,256]{2,1,0:T(8,128)S(1)}, f32[4,64,256]{2,1,0:T(8,128)S(1)}, u32[]{:S(2)}, u32[]{:S(2)}) collective-permute-start(f32[4,64,256]{2,1,0:T(8,128)S(1)} %shard_map.89.refs_1_.n1.refs_0_), channel_id=1, source_target_pairs={{1,2},{3,4},{5,6},{7,8},{9,10},{11,12},{13,14},{15,16},{17,18},{19... | collective-permute-start | bytes 786440 | tf_op jit(solution)/shard_map/ppermute | solution.py:298
  43.0 14.9 %collective-permute-start.7 = (f32[4,64,256]{2,1,0:T(8,128)S(1)}, f32[4,64,256]{2,1,0:T(8,128)S(1)}, u32[]{:S(2)}, u32[]{:S(2)}) collective-permute-start(f32[4,64,256]{2,1,0:T(8,128)S(1)} %get-tuple-element.34.n2.refs_1_), channel_id=1, source_target_pairs={{1,2},{3,4},{5,6},{7,8},{9,10},{11,12},{13,14},{15,16},{17,18},{19... | collective-permute-start | bytes 786440 | tf_op jit(solution)/shard_map/ppermute | solution.py:298
  48.6 13.0 %collective-permute-start.8 = (f32[4,128,256]{2,1,0:T(8,128)S(1)}, f32[4,128,256]{2,1,0:T(8,128)S(1)}, u32[]{:S(2)}, u32[]{:S(2)}) collective-permute-start(f32[4,128,256]{2,1,0:T(8,128)S(1)} %get-tuple-element.42.refs_2_), channel_id=1, source_target_pairs={{0,1},{1,0},{2,3},{3,2},{4,5},{5,4},{6,7},{7,6},{8,9},{9,8},{10,11... | collective-permute-start | bytes 1572872 | tf_op jit(solution)/shard_map/ppermute | solution.py:345
  50.6 15.0 %collective-permute-start.9 = (f32[4,64,256]{2,1,0:T(8,128)S(1)}, f32[4,64,256]{2,1,0:T(8,128)S(1)}, u32[]{:S(2)}, u32[]{:S(2)}) collective-permute-start(f32[4,64,256]{2,1,0:T(8,128)S(1)} %shard_map.92.refs_1_.n1), channel_id=1, source_target_pairs={{1,2},{3,4},{5,6},{7,8},{9,10},{11,12},{13,14},{15,16},{17,18},{19... | collective-permute-start | bytes 786440 | tf_op jit(solution)/shard_map/ppermute | solution.py:298
  58.0 14.8 %collective-permute-start.10 = (f32[4,64,256]{2,1,0:T(8,128)S(1)}, f32[4,64,256]{2,1,0:T(8,128)S(1)}, u32[]{:S(2)}, u32[]{:S(2)}) collective-permute-start(f32[4,64,256]{2,1,0:T(8,128)S(1)} %get-tuple-element.40.n2), channel_id=1, source_target_pairs={{1,2},{3,4},{5,6},{7,8},{9,10},{11,12},{13,14},{15,16},{17,18},{19... | collective-permute-start | bytes 786440 | tf_op jit(solution)/shard_map/ppermute | solution.py:298
  63.2 9.6 %collective-permute-start.11 = (f32[4,128,256]{2,1,0:T(8,128)S(1)}, f32[4,128,256]{2,1,0:T(8,128)S(1)}, u32[]{:S(2)}, u32[]{:S(2)}) collective-permute-start(f32[4,128,256]{2,1,0:T(8,128)S(1)} %get-tuple-element.44.na), channel_id=1, source_target_pairs={{0,1},{1,0},{2,3},{3,2},{4,5},{5,4},{6,7},{7,6},{8,9},{9,8},{10,11... | collective-permute-start | bytes 1572872 | tf_op jit(solution)/shard_map/ppermute | solution.py:345
  74.4 17.1 %all-to-all-start = ((f32[8,4,8,8,128]{4,3,2,1,0:T(8,128)}), f32[8,4,8,8,128]{4,3,2,1,0:T(8,128)S(1)}, u32[]{:S(2)}, u32[]{:S(2)}) async-start(f32[8,4,8,8,128]{4,3,2,1,0:T(8,128)} %get-tuple-element.50), calls=%async_computation | async-start | bytes 2097152 | tf_op jit(solution)/shard_map/all_to_all | solution.py:361
  80.3 11.2 %copy-start.3 = (f32[8,8,128]{2,1,0:T(8,128)S(1)}, f32[8,8,128]{2,1,0:T(8,128)}, u32[]{:S(2)}) copy-start(f32[8,8,128]{2,1,0:T(8,128)} %image.1) | copy-start | bytes 98308

commit v3 on v2

--- a/solution.py
+++ b/solution.py
@@ -13,8 +13,8 @@
 TAPS = (8064.0, -1008.0, 128.0, -9.0)
 PLANES, NY, NZ = 8, 128, 256
 FACE = 4
-HALVES = 2
-ROWS = NY // HALVES
+FIRST = (0, 64)
+ROWS = (64, 64)
 ZY, ZZ = 64, 128
 GROUPS = 8
 VMEM_LIMIT = 16 * 1024 * 1024
@@ -80,19 +80,24 @@
     return along_z + along_y
 
 
+def slab_terms(values, j, total):
+    total = total + CENTRE * values[j]
+    for k, tap in enumerate(TAPS, 1):
+        pair = [values[i] for i in (j + k, j - k) if 0 <= i < len(values)]
+        if pair:
+            total = total + tap * sum(pair[1:], pair[0])
+    return total
+
+
 def advance(now, older, coef_of, cross, store_base, store_next):
-    for half in range(HALVES):
-        for block in range(ROWS // 8):
+    for half in range(len(ROWS)):
+        for block in range(ROWS[half] // 8):
             inner = pl.ds(block * 8, 8)
-            outer = pl.ds(half * ROWS + block * 8, 8)
+            outer = pl.ds(FIRST[half] + block * 8, 8)
             at = (inner, outer, half)
             values = [now(j, at) for j in range(PLANES)]
             for j in range(PLANES):
-                total = cross[j, outer, :] + CENTRE * values[j]
-                for k, tap in enumerate(TAPS, 1):
-                    pair = [values[i] for i in (j + k, j - k) if 0 <= i < len(values)]
-                    if pair:
-                        total = total + tap * sum(pair[1:], pair[0])
+                total = slab_terms(values, j, cross[j, outer, :])
                 value = 2.0 * values[j] - older(j, at) + coef_of(j, at) * total
                 if j < FACE:
                     store_base(j, at, value)
@@ -139,57 +144,54 @@
     return put
 
 
-def first_kernel(
-    table_ref, now, prev, regions, coef, base, rest, cross, across_y, across_z, table, sem
-):
+def first_kernel(now, total, across_y, across_z):
+    flip = flip_of()
+    store_bands(across_y, across_z)
+    for j in range(PLANES):
+        total[j] = cross_terms(now[j ^ flip], across_y[...], across_z[...])
+    for block in range(NY // 8):
+        rows = pl.ds(block * 8, 8)
+        values = [now[j ^ flip, rows, :] for j in range(PLANES)]
+        for j in range(PLANES):
+            total[j, rows, :] = slab_terms(values, j, total[j, rows, :])
+
+
+def second_kernel(table_ref, now, prev, regions, total, coef, base, rest, table, sem):
     load = pltpu.make_async_copy(table_ref, table, sem)
     load.start()
     flip = flip_of()
-    store_bands(across_y, across_z)
-    for j in range(PLANES):
-        cross[j] = cross_terms(now[j ^ flip], across_y[...], across_z[...])
     load.wait()
     scaled = [table[i] * (1.0 / SCALE) for i in range(16)]
-
-    def coef_of(j, at):
-        code = regions[j ^ flip, at[1], :]
-        level = scaled
-        for bit in range(4):
-            odd = (code & (1 << bit)) != 0
-            level = [
-                jnp.where(odd, level[2 * i + 1], level[2 * i]) for i in range(len(level) // 2)
-            ]
-        coef[j, at[1], :] = level[0]
-        return level[0]
-
-    advance(
-        from_natural(now, flip),
-        from_natural(prev, flip),
-        coef_of,
-        cross,
-        put_rows(base),
-        put_rows(rest),
-    )
-
-
-def middle_kernel(first, box_ref, n1, n2, partial, halo, *refs):
-    *refs, now, base, nxt, zones, cross, across_y, across_z = refs
-    box = first_cell(box_ref)
+    for j in range(PLANES):
+        for block in range(NY // 8):
+            rows = pl.ds(block * 8, 8)
+            code = regions[j ^ flip, rows, :]
+            level = scaled
+            for bit in range(4):
+                odd = (code & (1 << bit)) != 0
+                level = [
+                    jnp.where(odd, level[2 * i + 1], level[2 * i]) for i in range(len(level) // 2)
+                ]
+            coef[j, rows, :] = level[0]
+            value = 2.0 * now[j ^ flip, rows, :] - prev[j ^ flip, rows, :] + level[0] * total[j, rows, :]
+            if j < FACE:
+                base[j, rows, :] = value
+            else:
+                rest[j - FACE, rows, :] = value
+
+
+def middle_kernel(first, n1, n2, partial, halo, *refs):
+    *refs, now, base, nxt, cross, across_y, across_z = refs
     if first:
         prev, coef = refs
         older = from_natural(prev, flip_of())
-        earlier = ()
     else:
-        p1, p2, pa, coef, *earlier = refs
+        p1, p2, pa, coef = refs
         older = from_parts(p1, p2, pa)
-    for zone in earlier:
-        zones[:, : zone.shape[1]] = zone[...]
     far_terms(coef, partial, halo, 3 & ~flip_of() if first else 0, now)
     store_bands(across_y, across_z)
     for j in range(PLANES):
         cross[j] = cross_terms(whole_plane(n1, n2, now, j), across_y[...], across_z[...])
-    for j in range(PLANES):
-        zones[:, zones.shape[1] - 1, j] = split_zone(whole_plane(n1, n2, now, j), box)
     advance(
         from_parts(n1, n2, now),
         older,
@@ -201,9 +203,9 @@
 
 
 def face_terms(base, coef, halo, turn, half, put):
-    for block in range(ROWS // 8):
+    for block in range(ROWS[half] // 8):
         inner = pl.ds(block * 8, 8)
-        outer = pl.ds(half * ROWS + block * 8, 8)
+        outer = pl.ds(FIRST[half] + block * 8, 8)
         beyond = [halo[k ^ turn, inner, :] for k in range(FACE)]
         for j in range(FACE):
             total = TAPS[j] * beyond[0]
@@ -234,27 +236,46 @@
             out[mine, rows, :] = partial[mine, rows, :] + coef[FACE + mine, rows, :] * total
 
 
+def store_zones(box_ref, pieces, held, sems, zones, step):
+    box = first_cell(box_ref)
+    for j in range(PLANES):
+        held[:, step % held.shape[1], j] = split_zone(whole_plane(*pieces, j), box)
+    copy = pltpu.make_async_copy(
+        held.at[:, step % held.shape[1]], zones.at[:, step], sems.at[step % held.shape[1]]
+    )
+    copy.start()
+    return copy
+
+
+def zones_kernel(box_ref, *refs):
+    *pieces, zones, held, sems = refs
+    copies = [
+        store_zones(box_ref, pieces[3 * step : 3 * step + 3], held, sems, zones, step)
+        for step in range(STEPS - 1)
+    ]
+    for copy in copies:
+        copy.wait()
+
+
 def last_kernel(
-    box_ref, base, coef, halo, n1, partial, far_halo, earlier, n2, now, zones
+    box_ref, base, coef, halo, n1, partial, far_halo, earlier, n2, now, zones, held, sems
 ):
-    box = first_cell(box_ref)
+    del earlier
 
     def put(j, inner, value):
         n2[j, inner, :] = value
 
     face_terms(base, coef, halo, 0, 1, put)
     far_terms(coef, partial, far_halo, 0, now)
-    zones[:, : STEPS - 1] = earlier[...]
-    for j in range(PLANES):
-        zones[:, STEPS - 1, j] = split_zone(whole_plane(n1, n2, now, j), box)
+    store_zones(box_ref, (n1, n2, now), held, sems, zones, STEPS - 1).wait()
 
 
 def gather_kernel(n1, n2, na, out, sems):
     flip = flip_of()
     copies = []
     for j in range(FACE):
-        copies.append((n1.at[j], out.at[j ^ flip, pl.ds(0, ROWS)]))
-        copies.append((n2.at[j], out.at[j ^ flip, pl.ds(ROWS, ROWS)]))
+        copies.append((n1.at[j], out.at[j ^ flip, pl.ds(FIRST[0], ROWS[0])]))
+        copies.append((n2.at[j], out.at[j ^ flip, pl.ds(FIRST[1], ROWS[1])]))
         copies.append((na.at[j], out.at[(j + FACE) ^ flip]))
     copies = [
         pltpu.make_async_copy(source, target, sems.at[i])
@@ -286,7 +307,7 @@
     inside = [(i, i ^ 1) for i in range(count)]
     across = [(i, i + 1) for i in range(1, count - 1, 2)]
     across = across + [(j, i) for i, j in across]
-    half_shape = (FACE, ROWS, NZ)
+    part_shapes = [(FACE, rows, NZ) for rows in ROWS]
     face_shape = (FACE, NY, NZ)
     slab_shape = (PLANES, NY, NZ)
     zone_rows = (ZY // GROUPS, ZZ)
@@ -298,32 +319,41 @@
         return [lax.ppermute(half, "space", across) for half in halves]
 
     beyond = swap_faces(
-        lax.dynamic_slice(now, (4 * odd, half * ROWS, 0), half_shape) for half in range(HALVES)
+        lax.dynamic_slice(now, (4 * odd, first, 0), shape)
+        for first, shape in zip(FIRST, part_shapes)
     )
     halo = lax.ppermute(
         lax.dynamic_slice(now, (4 - 4 * odd, 0, 0), face_shape), "space", inside
     )
+    total = call(
+        first_kernel,
+        [slab_shape],
+        [VM],
+        [VM],
+        (now,),
+        scratch=work[1:],
+    )[0]
     coef, base, rest = call(
-        first_kernel,
+        second_kernel,
         [slab_shape] + [face_shape] * 2,
-        [ANY] + [VM] * 3,
+        [ANY] + [VM] * 4,
         [VM] * 3,
-        (speed_table, now, prev, regions),
-        scratch=work + [pltpu.SMEM(speed_table.shape, F32), pltpu.SemaphoreType.DMA(())],
+        (speed_table, now, prev, regions, total),
+        scratch=[pltpu.SMEM(speed_table.shape, F32), pltpu.SemaphoreType.DMA(())],
     )
     older = [now]
-    zones = ()
+    levels = ()
     for step in range(STEPS - 1):
         n1 = call(
             functools.partial(face_kernel, 0, step == 0),
-            [half_shape],
+            part_shapes[:1],
             [VM] * 3,
             [VM],
             (base, coef, beyond[0]),
         )[0]
         n2, rest = call(
             functools.partial(face_kernel, 1, step == 0),
-            [half_shape, face_shape],
+            [part_shapes[1], face_shape],
             [VM] * 3 + [ANY] * 2,
             [VM, ANY],
             (base, coef, beyond[1], rest, n1),
@@ -331,34 +361,50 @@
             aliases={3: 1},
         )
         beyond = swap_faces([n1, n2])
-        full, base, rest, zone = call(
+        full, base, rest = call(
             functools.partial(middle_kernel, step == 0),
-            [face_shape] * 3 + [(GROUPS, step + 1, PLANES) + zone_rows],
-            [VM] * (6 + len(older) + len(zones)),
-            [VM] * 4,
-            (box, n1, n2, rest, halo, *older, coef, *zones),
+            [face_shape] * 3,
+            [VM] * (5 + len(older)),
+            [VM] * 3,
+            (n1, n2, rest, halo, *older, coef),
             cost=COST[0] if step < STEPS - 2 else COST[2],
             scratch=work,
         )
-        zones = (zone,)
         older = (n1, n2, full)
+        levels += older
         halo = lax.ppermute(full, "space", inside)
     n1 = call(
         functools.partial(face_kernel, 0, False),
-        [half_shape],
+        part_shapes[:1],
         [VM] * 3,
         [VM],
         (base, coef, beyond[0]),
         cost=COST[3],
     )[0]
-    n2, full, zone = call(
+    zones = call(
+        zones_kernel,
+        [(GROUPS, STEPS, PLANES) + zone_rows],
+        [VM] * (1 + len(levels)),
+        [ANY],
+        (box, *levels),
+        scratch=[
+            pltpu.VMEM((GROUPS, STEPS - 1, PLANES) + zone_rows, F32),
+            pltpu.SemaphoreType.DMA((STEPS - 1,)),
+        ],
+    )[0]
+    n2, full, zones = call(
         last_kernel,
-        [half_shape, face_shape, (GROUPS, STEPS, PLANES) + zone_rows],
-        [VM] * 8,
-        [VM] * 3,
-        (box, base, coef, beyond[1], n1, rest, halo, zone),
-    )
-    received = lax.all_to_all(zone, "group", split_axis=0, concat_axis=0, tiled=True)
+        [part_shapes[1], face_shape, zones.shape],
+        [VM] * 7 + [ANY],
+        [VM] * 2 + [ANY],
+        (box, base, coef, beyond[1], n1, rest, halo, zones),
+        aliases={7: 2},
+        scratch=[
+            pltpu.VMEM((GROUPS, 1, PLANES) + zone_rows, F32),
+            pltpu.SemaphoreType.DMA((1,)),
+        ],
+    )
+    received = lax.all_to_all(zones, "group", split_axis=0, concat_axis=0, tiled=True)
 
     def gather(three):
         return call(

time: 92.7 us -> 92.5 us (level)
  Pallas kernels: 11.6 us -> 13.3 us
  local copies, waits for them, and re-layouts: 3.22 us -> 2.04 us
    pallas_call x15 -> x17, Pallas kernels: 11.6 us -> 13.3 us  [call(): pl.pallas_call(kernel, out_shape=[jax.ShapeDtypeStruct(shape, F32) for sh...]
    unnamed x12, local copies, waits for them, and re-layouts: 1.89 us -> 0.76 us
    ppermute x8, waiting for transfers between devices: 10.6 us -> 9.61 us  [swap_faces(): return [lax.ppermute(half, 'space', across) for half in halves]]
  transfers between devices with their start and end apart: 13 -> 13, of which waited for: 6 -> 5; matrix products, arithmetic and copies ran while one was open for 0% -> 0% of each run, Pallas kernels for 10% -> 12%
where the time goes in v3:
time: 92.5 us; the launch traced here: 92 us
  starting transfers between devices  55.8 us (60%)
  waiting for transfers between devices  19.9 us (22%)
  Pallas kernels  13.3 us (14%)
  local copies, waits for them, and re-layouts  2.04 us (2%)
  between operations  0.98 us (1%)
    ppermute x8, starting transfers between devices, swap_faces(): return [lax.ppermute(half, 'space', across) for half in halves]  42.6 us
    pallas_call x17, Pallas kernels, call(): pl.pallas_call(kernel, out_shape=[jax.ShapeDtypeStruct(shape, F32) for sh...  13.3 us
    all_to_all x1, waiting for transfers between devices, local(): lax.all_to_all(zones, 'group', split_axis=0, concat_axis=0, tiled=True)  10.3 us
    ppermute x8, waiting for transfers between devices, swap_faces(): return [lax.ppermute(half, 'space', across) for half in halves]  9.61 us
    ppermute x3, starting transfers between devices, local(): halo = lax.ppermute(full, 'space', inside)  5.76 us
    all_to_all x1, starting transfers between devices, local(): lax.all_to_all(zones, 'group', split_axis=0, concat_axis=0, tiled=True)  5.45 us
    ppermute x1, starting transfers between devices, local(): lax.ppermute(lax.dynamic_slice(now, (4 - 4 * odd, 0, 0), face_shape), 'sp...  1.92 us
  transfers between devices with their start and end apart: 13, of which 5 were waited for; matrix products, arithmetic and copies ran while one was open for 0% of the time, Pallas kernels for 12%

profile of v3, /device:TPU:32, one launch (start us, length us, event | category | flops | bytes accessed | tf_op | source)
XLA Modules:
  0.0 92.0 jit_solution(15961292648022765358)
XLA Ops:
  0.6 1.2 %dynamic-slice_bitcast_fusion.1 = (f32[4,64,256]{2,1,0:T(8,128)S(1)}, f32[4,64,256]{2,1,0:T(8,128)S(1)}) fusion(f32[1,8,128,256]{3,2,1,0:T(8,128)} %param.7, s32[]{:T(128)S(6)} %select_n.7), kind=kLoop, calls=%fused_computation.1 | loop fusion | bytes 1048580 | tf_op jit(solution)/shard_map/dynamic_slice | solution.py:322
  1.8 10.3 %collective-permute-start = (f32[4,64,256]{2,1,0:T(8,128)S(1)}, f32[4,64,256]{2,1,0:T(8,128)S(1)}, u32[]{:S(2)}, u32[]{:S(2)}) collective-permute-start(f32[4,64,256]{2,1,0:T(8,128)S(1)} %get-tuple-element.46), channel_id=1, source_target_pairs={{1,2},{3,4},{5,6},{7,8},{9,10},{11,12},{13,14},{15,16},{17,18},{19... | collective-permute-start | bytes 786440 | tf_op jit(solution)/shard_map/ppermute | solution.py:319
  12.1 1.9 %collective-permute-start.1 = (f32[4,64,256]{2,1,0:T(8,128)S(1)}, f32[4,64,256]{2,1,0:T(8,128)S(1)}, u32[]{:S(2)}, u32[]{:S(2)}) collective-permute-start(f32[4,64,256]{2,1,0:T(8,128)S(1)} %get-tuple-element.45), channel_id=1, source_target_pairs={{1,2},{3,4},{5,6},{7,8},{9,10},{11,12},{13,14},{15,16},{17,18},{19... | collective-permute-start | bytes 786440 | tf_op jit(solution)/shard_map/ppermute | solution.py:319
  14.1 1.9 %collective-permute-start.2 = (f32[4,128,256]{2,1,0:T(8,128)S(1)}, f32[4,128,256]{2,1,0:T(8,128)S(1)}, u32[]{:S(2)}, u32[]{:S(2)}) collective-permute-start(f32[4,128,256]{2,1,0:T(8,128)S(1)} %dynamic-slice_bitcast_fusion), channel_id=1, source_target_pairs={{0,1},{1,0},{2,3},{3,2},{4,5},{5,4},{6,7},{7,6},{8,9},{9,8},{10,11... | collective-permute-start | bytes 1572872 | tf_op jit(solution)/shard_map/ppermute | solution.py:325
  16.0 1.2 %shard_map.85.total = f32[8,128,256]{2,1,0:T(8,128)S(1)} custom-call(f32[8,128,256]{2,1,0:T(8,128)S(1)} %bitcast.10), custom_call_target="tpu_custom_call" | custom-call | flops 1 | bytes 1 | tf_op jit(solution)/shard_map/pallas_call | solution.py:48
  17.2 0.3 copy-done.2
  17.6 0.4 copy-done.4
  18.0 1.5 %shard_map.86 = (f32[8,128,256]{2,1,0:T(8,128)S(1)}, f32[4,128,256]{2,1,0:T(8,128)S(1)}, f32[4,128,256]{2,1,0:T(8,128)S(1)}) custom-call(f32[16]{0:T(128)S(1)} %copy-done.4, f32[8,128,256]{2,1,0:T(8,128)S(1)} %bitcast.11, f32[8,128,256]{2,1,0:T(8,128)S(1)} %bitcast.13, s32[8,128,256]{2,1,0:T(8,128)S(1)} %copy-done.2, f32[8,128,256]{2,1,0:T(8,128)S(1)} %shard_map.85.total), custom_call_target="tpu_custom_call" | custom-call | flops 1 | bytes 1 | tf_op jit(solution)/shard_map/pallas_call | solution.py:48
  19.5 7.9 %collective-permute-start.3 = (f32[4,64,256]{2,1,0:T(8,128)S(1)}, f32[4,64,256]{2,1,0:T(8,128)S(1)}, u32[]{:S(2)}, u32[]{:S(2)}) collective-permute-start(f32[4,64,256]{2,1,0:T(8,128)S(1)} %shard_map.87.refs_1_.n1.refs_0_), channel_id=1, source_target_pairs={{1,2},{3,4},{5,6},{7,8},{9,10},{11,12},{13,14},{15,16},{17,18},{19... | collective-permute-start | bytes 786440 | tf_op jit(solution)/shard_map/ppermute | solution.py:319
  27.4 0.1 shard_map.88
  27.5 3.7 %collective-permute-start.4 = (f32[4,64,256]{2,1,0:T(8,128)S(1)}, f32[4,64,256]{2,1,0:T(8,128)S(1)}, u32[]{:S(2)}, u32[]{:S(2)}) collective-permute-start(f32[4,64,256]{2,1,0:T(8,128)S(1)} %get-tuple-element.27.n2.refs_1_), channel_id=1, source_target_pairs={{1,2},{3,4},{5,6},{7,8},{9,10},{11,12},{13,14},{15,16},{17,18},{19... | collective-permute-start | bytes 786440 | tf_op jit(solution)/shard_map/ppermute | solution.py:319
  31.3 1.3 %shard_map.89 = (f32[4,128,256]{2,1,0:T(8,128)S(1)}, f32[4,128,256]{2,1,0:T(8,128)S(1)}, f32[4,128,256]{2,1,0:T(8,128)S(1)}) custom-call(f32[4,64,256]{2,1,0:T(8,128)S(1)} %shard_map.87.refs_1_.n1.refs_0_, f32[4,64,256]{2,1,0:T(8,128)S(1)} %get-tuple-element.27.n2.refs_1_, f32[4,128,256]{2,1,0:T(8,128)S(1)} %get-tuple-element.28.partial, ...), custom_call_target="tpu_custom_call" | custom-call | flops 1 | bytes 1 | tf_op jit(solution)/shard_map/pallas_call | solution.py:48
  32.6 1.6 %collective-permute-done.3.halo = f32[4,64,256]{2,1,0:T(8,128)S(1)} collective-permute-done((f32[4,64,256]{2,1,0:T(8,128)S(1)}, f32[4,64,256]{2,1,0:T(8,128)S(1)}, u32[]{:S(2)}, u32[]{:S(2)}) %collective-permute-start.3) | collective-permute-done | bytes 262176 | tf_op jit(solution)/shard_map/ppermute | solution.py:319
  34.3 6.4 %collective-permute-start.6 = (f32[4,64,256]{2,1,0:T(8,128)S(1)}, f32[4,64,256]{2,1,0:T(8,128)S(1)}, u32[]{:S(2)}, u32[]{:S(2)}) collective-permute-start(f32[4,64,256]{2,1,0:T(8,128)S(1)} %shard_map.90.refs_1_.n1.refs_0_.refs_3_), channel_id=1, source_target_pairs={{1,2},{3,4},{5,6},{7,8},{9,10},{11,12},{13,14},{15,16},{17,18},{19... | collective-permute-start | bytes 786440 | tf_op jit(solution)/shard_map/ppermute | solution.py:319
  40.7 1.9 %collective-permute-start.5 = (f32[4,128,256]{2,1,0:T(8,128)S(1)}, f32[4,128,256]{2,1,0:T(8,128)S(1)}, u32[]{:S(2)}, u32[]{:S(2)}) collective-permute-start(f32[4,128,256]{2,1,0:T(8,128)S(1)} %get-tuple-element.33.refs_2_), channel_id=1, source_target_pairs={{0,1},{1,0},{2,3},{3,2},{4,5},{5,4},{6,7},{7,6},{8,9},{9,8},{10,11... | collective-permute-start | bytes 1572872 | tf_op jit(solution)/shard_map/ppermute | solution.py:375
  42.7 3.8 %collective-permute-start.7 = (f32[4,64,256]{2,1,0:T(8,128)S(1)}, f32[4,64,256]{2,1,0:T(8,128)S(1)}, u32[]{:S(2)}, u32[]{:S(2)}) collective-permute-start(f32[4,64,256]{2,1,0:T(8,128)S(1)} %get-tuple-element.31.n2.refs_1_.refs_4_), channel_id=1, source_target_pairs={{1,2},{3,4},{5,6},{7,8},{9,10},{11,12},{13,14},{15,16},{17,18},{19... | collective-permute-start | bytes 786440 | tf_op jit(solution)/shard_map/ppermute | solution.py:319
  46.6 1.3 %shard_map.92 = (f32[4,128,256]{2,1,0:T(8,128)S(1)}, f32[4,128,256]{2,1,0:T(8,128)S(1)}, f32[4,128,256]{2,1,0:T(8,128)S(1)}) custom-call(f32[4,64,256]{2,1,0:T(8,128)S(1)} %shard_map.90.refs_1_.n1.refs_0_.refs_3_, f32[4,64,256]{2,1,0:T(8,128)S(1)} %get-tuple-element.31.n2.refs_1_.refs_4_, f32[4,128,256]{2,1,0:T(8,128)S(1)} %get-tuple-element.32.partial, ...), custom_call_target="tpu_custom_call" | custom-call | flops 1 | bytes 1 | tf_op jit(solution)/shard_map/pallas_call | solution.py:48
  47.9 1.2 %collective-permute-done.6.halo = f32[4,64,256]{2,1,0:T(8,128)S(1)} collective-permute-done((f32[4,64,256]{2,1,0:T(8,128)S(1)}, f32[4,64,256]{2,1,0:T(8,128)S(1)}, u32[]{:S(2)}, u32[]{:S(2)}) %collective-permute-start.6) | collective-permute-done | bytes 262176 | tf_op jit(solution)/shard_map/ppermute | solution.py:319
  49.2 4.8 %collective-permute-start.9 = (f32[4,64,256]{2,1,0:T(8,128)S(1)}, f32[4,64,256]{2,1,0:T(8,128)S(1)}, u32[]{:S(2)}, u32[]{:S(2)}) collective-permute-start(f32[4,64,256]{2,1,0:T(8,128)S(1)} %shard_map.93.refs_1_.n1.refs_6_), channel_id=1, source_target_pairs={{1,2},{3,4},{5,6},{7,8},{9,10},{11,12},{13,14},{15,16},{17,18},{19... | collective-permute-start | bytes 786440 | tf_op jit(solution)/shard_map/ppermute | solution.py:319
  54.0 1.9 %collective-permute-start.8 = (f32[4,128,256]{2,1,0:T(8,128)S(1)}, f32[4,128,256]{2,1,0:T(8,128)S(1)}, u32[]{:S(2)}, u32[]{:S(2)}) collective-permute-start(f32[4,128,256]{2,1,0:T(8,128)S(1)} %get-tuple-element.38.refs_2_.refs_5_), channel_id=1, source_target_pairs={{0,1},{1,0},{2,3},{3,2},{4,5},{5,4},{6,7},{7,6},{8,9},{9,8},{10,11... | collective-permute-start | bytes 1572872 | tf_op jit(solution)/shard_map/ppermute | solution.py:375
  55.9 1.1 %collective-permute-done.7.halo = f32[4,64,256]{2,1,0:T(8,128)S(1)} collective-permute-done((f32[4,64,256]{2,1,0:T(8,128)S(1)}, f32[4,64,256]{2,1,0:T(8,128)S(1)}, u32[]{:S(2)}, u32[]{:S(2)}) %collective-permute-start.7) | collective-permute-done | bytes 262176 | tf_op jit(solution)/shard_map/ppermute | solution.py:319
  57.1 3.9 %collective-permute-start.10 = (f32[4,64,256]{2,1,0:T(8,128)S(1)}, f32[4,64,256]{2,1,0:T(8,128)S(1)}, u32[]{:S(2)}, u32[]{:S(2)}) collective-permute-start(f32[4,64,256]{2,1,0:T(8,128)S(1)} %get-tuple-element.36.n2.refs_7_), channel_id=1, source_target_pairs={{1,2},{3,4},{5,6},{7,8},{9,10},{11,12},{13,14},{15,16},{17,18},{19... | collective-permute-start | bytes 786440 | tf_op jit(solution)/shard_map/ppermute | solution.py:319
  61.0 1.3 %shard_map.95 = (f32[4,128,256]{2,1,0:T(8,128)S(1)}, f32[4,128,256]{2,1,0:T(8,128)S(1)}, f32[4,128,256]{2,1,0:T(8,128)S(1)}) custom-call(f32[4,64,256]{2,1,0:T(8,128)S(1)} %shard_map.93.refs_1_.n1.refs_6_, f32[4,64,256]{2,1,0:T(8,128)S(1)} %get-tuple-element.36.n2.refs_7_, f32[4,128,256]{2,1,0:T(8,128)S(1)} %get-tuple-element.37.partial, ...), custom_call_target="tpu_custom_call" | custom-call | flops 1 | bytes 1 | tf_op jit(solution)/shard_map/pallas_call | solution.py:48
  62.4 1.9 %collective-permute-start.11 = (f32[4,128,256]{2,1,0:T(8,128)S(1)}, f32[4,128,256]{2,1,0:T(8,128)S(1)}, u32[]{:S(2)}, u32[]{:S(2)}) collective-permute-start(f32[4,128,256]{2,1,0:T(8,128)S(1)} %get-tuple-element.39.na.refs_8_), channel_id=1, source_target_pairs={{0,1},{1,0},{2,3},{3,2},{4,5},{5,4},{6,7},{7,6},{8,9},{9,8},{10,11... | collective-permute-start | bytes 1572872 | tf_op jit(solution)/shard_map/ppermute | solution.py:375
  64.5 2.0 %shard_map.98.earlier = f32[8,4,8,8,128]{4,3,2,1,0:T(8,128)} custom-call(f32[2,8,128]{2,1,0:T(8,128)S(1)} %broadcast_in_dim.13.box_ref, f32[4,64,256]{2,1,0:T(8,128)S(1)} %shard_map.87.refs_1_.n1.refs_0_, f32[4,64,256]{2,1,0:T(8,128)S(1)} %get-tuple-element.27.n2.refs_1_, f32[4,128,256]{2,1,0:T(8,128)S(1)} %get-tuple-element.33.refs_2_, ...), custom_call_target="tpu_custom_call" | custom-call | flops 1 | bytes 1 | tf_op jit(solution)/shard_map/pallas_call | solution.py:48
  66.5 5.6 %collective-permute-done.10.halo = f32[4,64,256]{2,1,0:T(8,128)S(1)} collective-permute-done((f32[4,64,256]{2,1,0:T(8,128)S(1)}, f32[4,64,256]{2,1,0:T(8,128)S(1)}, u32[]{:S(2)}, u32[]{:S(2)}) %collective-permute-start.10) | collective-permute-done | bytes 262176 | tf_op jit(solution)/shard_map/ppermute | solution.py:319
  72.1 1.3 %shard_map.99 = (f32[4,64,256]{2,1,0:T(8,128)S(1)}, f32[4,128,256]{2,1,0:T(8,128)S(1)}, f32[8,4,8,8,128]{4,3,2,1,0:T(8,128)}) custom-call(f32[2,8,128]{2,1,0:T(8,128)S(1)} %broadcast_in_dim.13.box_ref, f32[4,128,256]{2,1,0:T(8,128)S(1)} %get-tuple-element.40.base, ...), custom_call_target="tpu_custom_call", output_to_operand_aliasing={{2}: (7, {})} | custom-call | flops 1 | bytes 1 | tf_op jit(solution)/shard_map/pallas_call | solution.py:48
  73.4 5.4 %all-to-all-start = ((f32[8,4,8,8,128]{4,3,2,1,0:T(8,128)}), f32[8,4,8,8,128]{4,3,2,1,0:T(8,128)S(1)}, u32[]{:S(2)}, u32[]{:S(2)}) async-start(f32[8,4,8,8,128]{4,3,2,1,0:T(8,128)} %get-tuple-element.44), calls=%async_computation | async-start | bytes 2097152 | tf_op jit(solution)/shard_map/all_to_all | solution.py:407
  78.9 1.1 %shard_map.96 = f32[8,128,256]{2,1,0:T(8,128)} custom-call(f32[4,64,256]{2,1,0:T(8,128)S(1)} %shard_map.93.refs_1_.n1.refs_6_, f32[4,64,256]{2,1,0:T(8,128)S(1)} %get-tuple-element.36.n2.refs_7_, f32[4,128,256]{2,1,0:T(8,128)S(1)} %get-tuple-element.39.na.refs_8_), custom_call_target="tpu_custom_call" | custom-call | flops 1 | bytes 1 | tf_op jit(solution)/shard_map/pallas_call | solution.py:48
  80.0 1.1 %shard_map.100 = f32[8,128,256]{2,1,0:T(8,128)} custom-call(f32[4,64,256]{2,1,0:T(8,128)S(1)} %shard_map.97.n1, f32[4,64,256]{2,1,0:T(8,128)S(1)} %get-tuple-element.42.n2, f32[4,128,256]{2,1,0:T(8,128)S(1)} %get-tuple-element.43.na), custom_call_target="tpu_custom_call" | custom-call | flops 1 | bytes 1 | tf_op jit(solution)/shard_map/pallas_call | solution.py:48
  81.0 10.3 %all-to-all-done.received = f32[8,4,8,8,128]{4,3,2,1,0:T(8,128)S(1)} async-done(((f32[8,4,8,8,128]{4,3,2,1,0:T(8,128)}), f32[8,4,8,8,128]{4,3,2,1,0:T(8,128)S(1)}, u32[]{:S(2)}, u32[]{:S(2)}) %all-to-all-start) | async-done | bytes 1048608 | tf_op jit(solution)/shard_map/all_to_all | solution.py:407
  91.4 0.7 shard_map.101
  (27 shorter events, 0.6 us)
Async XLA Ops:
  0.6 13.4 %copy-start = (f32[1,8,128,256]{3,2,1,0:T(8,128)S(1)}, f32[1,8,128,256]{3,2,1,0:T(8,128)}, u32[]{:S(2)}) copy-start(f32[1,8,128,256]{3,2,1,0:T(8,128)} %param.7) | copy-start | bytes 3145732
  1.8 17.6 %collective-permute-start = (f32[4,64,256]{2,1,0:T(8,128)S(1)}, f32[4,64,256]{2,1,0:T(8,128)S(1)}, u32[]{:S(2)}, u32[]{:S(2)}) collective-permute-start(f32[4,64,256]{2,1,0:T(8,128)S(1)} %get-tuple-element.46), channel_id=1, source_target_pairs={{1,2},{3,4},{5,6},{7,8},{9,10},{11,12},{13,14},{15,16},{17,18},{19... | collective-permute-start | bytes 786440 | tf_op jit(solution)/shard_map/ppermute | solution.py:319
  12.1 15.3 %collective-permute-start.1 = (f32[4,64,256]{2,1,0:T(8,128)S(1)}, f32[4,64,256]{2,1,0:T(8,128)S(1)}, u32[]{:S(2)}, u32[]{:S(2)}) collective-permute-start(f32[4,64,256]{2,1,0:T(8,128)S(1)} %get-tuple-element.45), channel_id=1, source_target_pairs={{1,2},{3,4},{5,6},{7,8},{9,10},{11,12},{13,14},{15,16},{17,18},{19... | collective-permute-start | bytes 786440 | tf_op jit(solution)/shard_map/ppermute | solution.py:319
  14.1 17.2 %collective-permute-start.2 = (f32[4,128,256]{2,1,0:T(8,128)S(1)}, f32[4,128,256]{2,1,0:T(8,128)S(1)}, u32[]{:S(2)}, u32[]{:S(2)}) collective-permute-start(f32[4,128,256]{2,1,0:T(8,128)S(1)} %dynamic-slice_bitcast_fusion), channel_id=1, source_target_pairs={{0,1},{1,0},{2,3},{3,2},{4,5},{5,4},{6,7},{7,6},{8,9},{9,8},{10,11... | collective-permute-start | bytes 1572872 | tf_op jit(solution)/shard_map/ppermute | solution.py:325
  16.0 1.2 %copy-start.1 = (f32[1,8,128,256]{3,2,1,0:T(8,128)S(1)}, f32[1,8,128,256]{3,2,1,0:T(8,128)}, u32[]{:S(2)}) copy-start(f32[1,8,128,256]{3,2,1,0:T(8,128)} %param.6) | copy-start | bytes 3145732
  16.0 1.5 %copy-start.2 = (s32[8,128,256]{2,1,0:T(8,128)S(1)}, s32[8,128,256]{2,1,0:T(8,128)}, u32[]{:S(2)}) copy-start(s32[8,128,256]{2,1,0:T(8,128)} %regions.1) | copy-start | bytes 3145732
  17.2 0.7 copy-start.4
  19.5 14.7 %collective-permute-start.3 = (f32[4,64,256]{2,1,0:T(8,128)S(1)}, f32[4,64,256]{2,1,0:T(8,128)S(1)}, u32[]{:S(2)}, u32[]{:S(2)}) collective-permute-start(f32[4,64,256]{2,1,0:T(8,128)S(1)} %shard_map.87.refs_1_.n1.refs_0_), channel_id=1, source_target_pairs={{1,2},{3,4},{5,6},{7,8},{9,10},{11,12},{13,14},{15,16},{17,18},{19... | collective-permute-start | bytes 786440 | tf_op jit(solution)/shard_map/ppermute | solution.py:319
  27.5 15.1 %collective-permute-start.4 = (f32[4,64,256]{2,1,0:T(8,128)S(1)}, f32[4,64,256]{2,1,0:T(8,128)S(1)}, u32[]{:S(2)}, u32[]{:S(2)}) collective-permute-start(f32[4,64,256]{2,1,0:T(8,128)S(1)} %get-tuple-element.27.n2.refs_1_), channel_id=1, source_target_pairs={{1,2},{3,4},{5,6},{7,8},{9,10},{11,12},{13,14},{15,16},{17,18},{19... | collective-permute-start | bytes 786440 | tf_op jit(solution)/shard_map/ppermute | solution.py:319
  34.3 14.8 %collective-permute-start.6 = (f32[4,64,256]{2,1,0:T(8,128)S(1)}, f32[4,64,256]{2,1,0:T(8,128)S(1)}, u32[]{:S(2)}, u32[]{:S(2)}) collective-permute-start(f32[4,64,256]{2,1,0:T(8,128)S(1)} %shard_map.90.refs_1_.n1.refs_0_.refs_3_), channel_id=1, source_target_pairs={{1,2},{3,4},{5,6},{7,8},{9,10},{11,12},{13,14},{15,16},{17,18},{19... | collective-permute-start | bytes 786440 | tf_op jit(solution)/shard_map/ppermute | solution.py:319
  40.7 5.9 %collective-permute-start.5 = (f32[4,128,256]{2,1,0:T(8,128)S(1)}, f32[4,128,256]{2,1,0:T(8,128)S(1)}, u32[]{:S(2)}, u32[]{:S(2)}) collective-permute-start(f32[4,128,256]{2,1,0:T(8,128)S(1)} %get-tuple-element.33.refs_2_), channel_id=1, source_target_pairs={{0,1},{1,0},{2,3},{3,2},{4,5},{5,4},{6,7},{7,6},{8,9},{9,8},{10,11... | collective-permute-start | bytes 1572872 | tf_op jit(solution)/shard_map/ppermute | solution.py:375
  42.7 3.8 %copy-start.5 = (s32[2]{0:T(128)S(1)}, s32[2]{0:T(128)}, u32[]{:S(2)}) copy-start(s32[2]{0:T(128)} %param.11) | copy-start | bytes 28
  42.7 14.3 %collective-permute-start.7 = (f32[4,64,256]{2,1,0:T(8,128)S(1)}, f32[4,64,256]{2,1,0:T(8,128)S(1)}, u32[]{:S(2)}, u32[]{:S(2)}) collective-permute-start(f32[4,64,256]{2,1,0:T(8,128)S(1)} %get-tuple-element.31.n2.refs_1_.refs_4_), channel_id=1, source_target_pairs={{1,2},{3,4},{5,6},{7,8},{9,10},{11,12},{13,14},{15,16},{17,18},{19... | collective-permute-start | bytes 786440 | tf_op jit(solution)/shard_map/ppermute | solution.py:319
  49.2 15.1 %collective-permute-start.9 = (f32[4,64,256]{2,1,0:T(8,128)S(1)}, f32[4,64,256]{2,1,0:T(8,128)S(1)}, u32[]{:S(2)}, u32[]{:S(2)}) collective-permute-start(f32[4,64,256]{2,1,0:T(8,128)S(1)} %shard_map.93.refs_1_.n1.refs_6_), channel_id=1, source_target_pairs={{1,2},{3,4},{5,6},{7,8},{9,10},{11,12},{13,14},{15,16},{17,18},{19... | collective-permute-start | bytes 786440 | tf_op jit(solution)/shard_map/ppermute | solution.py:319
  54.0 7.0 %collective-permute-start.8 = (f32[4,128,256]{2,1,0:T(8,128)S(1)}, f32[4,128,256]{2,1,0:T(8,128)S(1)}, u32[]{:S(2)}, u32[]{:S(2)}) collective-permute-start(f32[4,128,256]{2,1,0:T(8,128)S(1)} %get-tuple-element.38.refs_2_.refs_5_), channel_id=1, source_target_pairs={{0,1},{1,0},{2,3},{3,2},{4,5},{5,4},{6,7},{7,6},{8,9},{9,8},{10,11... | collective-permute-start | bytes 1572872 | tf_op jit(solution)/shard_map/ppermute | solution.py:375
  57.1 15.0 %collective-permute-start.10 = (f32[4,64,256]{2,1,0:T(8,128)S(1)}, f32[4,64,256]{2,1,0:T(8,128)S(1)}, u32[]{:S(2)}, u32[]{:S(2)}) collective-permute-start(f32[4,64,256]{2,1,0:T(8,128)S(1)} %get-tuple-element.36.n2.refs_7_), channel_id=1, source_target_pairs={{1,2},{3,4},{5,6},{7,8},{9,10},{11,12},{13,14},{15,16},{17,18},{19... | collective-permute-start | bytes 786440 | tf_op jit(solution)/shard_map/ppermute | solution.py:319
  62.4 9.8 %collective-permute-start.11 = (f32[4,128,256]{2,1,0:T(8,128)S(1)}, f32[4,128,256]{2,1,0:T(8,128)S(1)}, u32[]{:S(2)}, u32[]{:S(2)}) collective-permute-start(f32[4,128,256]{2,1,0:T(8,128)S(1)} %get-tuple-element.39.na.refs_8_), channel_id=1, source_target_pairs={{0,1},{1,0},{2,3},{3,2},{4,5},{5,4},{6,7},{7,6},{8,9},{9,8},{10,11... | collective-permute-start | bytes 1572872 | tf_op jit(solution)/shard_map/ppermute | solution.py:375
  73.4 17.9 %all-to-all-start = ((f32[8,4,8,8,128]{4,3,2,1,0:T(8,128)}), f32[8,4,8,8,128]{4,3,2,1,0:T(8,128)S(1)}, u32[]{:S(2)}, u32[]{:S(2)}) async-start(f32[8,4,8,8,128]{4,3,2,1,0:T(8,128)} %get-tuple-element.44), calls=%async_computation | async-start | bytes 2097152 | tf_op jit(solution)/shard_map/all_to_all | solution.py:407
  79.9 11.4 %copy-start.3 = (f32[8,8,128]{2,1,0:T(8,128)S(1)}, f32[8,8,128]{2,1,0:T(8,128)}, u32[]{:S(2)}) copy-start(f32[8,8,128]{2,1,0:T(8,128)} %image.1) | copy-start | bytes 98308

commit v4 on v3

--- a/solution.py
+++ b/solution.py
@@ -236,38 +236,40 @@
             out[mine, rows, :] = partial[mine, rows, :] + coef[FACE + mine, rows, :] * total
 
 
-def store_zones(box_ref, pieces, held, sems, zones, step):
+def zones_kernel(box_ref, coef, partial, far_halo, *refs):
+    *pieces, now, zones, held, sems = refs
     box = first_cell(box_ref)
-    for j in range(PLANES):
-        held[:, step % held.shape[1], j] = split_zone(whole_plane(*pieces, j), box)
-    copy = pltpu.make_async_copy(
-        held.at[:, step % held.shape[1]], zones.at[:, step], sems.at[step % held.shape[1]]
-    )
-    copy.start()
-    return copy
-
-
-def zones_kernel(box_ref, *refs):
-    *pieces, zones, held, sems = refs
-    copies = [
-        store_zones(box_ref, pieces[3 * step : 3 * step + 3], held, sems, zones, step)
-        for step in range(STEPS - 1)
-    ]
+    copies = []
+    for step in range(STEPS):
+        if step < STEPS - 1:
+            planes = [whole_plane(*pieces[3 * step : 3 * step + 3], j) for j in range(PLANES)]
+        else:
+            far_terms(coef, partial, far_halo, 0, now)
+            planes = [now[j] for j in range(FACE)]
+        cut = pl.ds(PLANES - len(planes), len(planes))
+        for j, plane in enumerate(planes, PLANES - len(planes)):
+            held[:, step, j] = split_zone(plane, box)
+        copies.append(
+            pltpu.make_async_copy(held.at[:, step, cut], zones.at[:, step, cut], sems.at[step])
+        )
+        copies[-1].start()
     for copy in copies:
         copy.wait()
 
 
-def last_kernel(
-    box_ref, base, coef, halo, n1, partial, far_halo, earlier, n2, now, zones, held, sems
-):
+def last_kernel(box_ref, base, coef, halo, n1, earlier, n2, zones, held, sem):
     del earlier
+    box = first_cell(box_ref)
 
     def put(j, inner, value):
         n2[j, inner, :] = value
 
     face_terms(base, coef, halo, 0, 1, put)
-    far_terms(coef, partial, far_halo, 0, now)
-    store_zones(box_ref, (n1, n2, now), held, sems, zones, STEPS - 1).wait()
+    for j in range(FACE):
+        held[:, j] = split_zone(jnp.concatenate([n1[j], n2[j]], axis=0), box)
+    copy = pltpu.make_async_copy(held, zones.at[:, STEPS - 1, pl.ds(0, FACE)], sem)
+    copy.start()
+    copy.wait()
 
 
 def gather_kernel(n1, n2, na, out, sems):
@@ -381,27 +383,25 @@
         (base, coef, beyond[0]),
         cost=COST[3],
     )[0]
-    zones = call(
+    zone_shape = (GROUPS, STEPS, PLANES) + zone_rows
+    full, zones = call(
         zones_kernel,
-        [(GROUPS, STEPS, PLANES) + zone_rows],
-        [VM] * (1 + len(levels)),
-        [ANY],
-        (box, *levels),
+        [face_shape, zone_shape],
+        [VM] * (4 + len(levels)),
+        [VM, ANY],
+        (box, coef, rest, halo, *levels),
+        scratch=[pltpu.VMEM(zone_shape, F32), pltpu.SemaphoreType.DMA((STEPS,))],
+    )
+    n2, zones = call(
+        last_kernel,
+        [part_shapes[1], zone_shape],
+        [VM] * 5 + [ANY],
+        [VM, ANY],
+        (box, base, coef, beyond[1], n1, zones),
+        aliases={5: 1},
         scratch=[
-            pltpu.VMEM((GROUPS, STEPS - 1, PLANES) + zone_rows, F32),
-            pltpu.SemaphoreType.DMA((STEPS - 1,)),
-        ],
-    )[0]
-    n2, full, zones = call(
-        last_kernel,
-        [part_shapes[1], face_shape, zones.shape],
-        [VM] * 7 + [ANY],
-        [VM] * 2 + [ANY],
-        (box, base, coef, beyond[1], n1, rest, halo, zones),
-        aliases={7: 2},
-        scratch=[
-            pltpu.VMEM((GROUPS, 1, PLANES) + zone_rows, F32),
-            pltpu.SemaphoreType.DMA((1,)),
+            pltpu.VMEM((GROUPS, FACE) + zone_rows, F32),
+            pltpu.SemaphoreType.DMA(()),
         ],
     )
     received = lax.all_to_all(zones, "group", split_axis=0, concat_axis=0, tiled=True)

time: 92.5 us -> 91.7 us (level)
    ppermute x8, waiting for transfers between devices: 9.61 us -> 7.81 us  [swap_faces(): return [lax.ppermute(half, 'space', across) for half in halves]]
    all_to_all x1, waiting for transfers between devices: 10.3 us -> 11.4 us  [local(): lax.all_to_all(zones, 'group', split_axis=0, concat_axis=0, tiled=True)]
    all_to_all x1, starting transfers between devices: 5.45 us -> 4.43 us  [local(): lax.all_to_all(zones, 'group', split_axis=0, concat_axis=0, tiled=True)]
  transfers between devices with their start and end apart: 13 -> 13, of which waited for: 5 -> 6; matrix products, arithmetic and copies ran while one was open for 0% -> 0% of each run, Pallas kernels for 12% -> 12%
where the time goes in v4:
time: 91.7 us; the launch traced here: 91.2 us
  starting transfers between devices  55.2 us (60%)
  waiting for transfers between devices  20.1 us (22%)
  Pallas kernels  12.8 us (14%)
  local copies, waits for them, and re-layouts  2.03 us (2%)
  between operations  0.98 us (1%)
    ppermute x8, starting transfers between devices, swap_faces(): return [lax.ppermute(half, 'space', across) for half in halves]  43.1 us
    pallas_call x17, Pallas kernels, call(): pl.pallas_call(kernel, out_shape=[jax.ShapeDtypeStruct(shape, F32) for sh...  12.8 us
    all_to_all x1, waiting for transfers between devices, local(): lax.all_to_all(zones, 'group', split_axis=0, concat_axis=0, tiled=True)  11.4 us
    ppermute x8, waiting for transfers between devices, swap_faces(): return [lax.ppermute(half, 'space', across) for half in halves]  7.81 us
    ppermute x3, starting transfers between devices, local(): halo = lax.ppermute(full, 'space', inside)  5.76 us
    all_to_all x1, starting transfers between devices, local(): lax.all_to_all(zones, 'group', split_axis=0, concat_axis=0, tiled=True)  4.43 us
    ppermute x1, starting transfers between devices, local(): lax.ppermute(lax.dynamic_slice(now, (4 - 4 * odd, 0, 0), face_shape), 'sp...  1.92 us
  transfers between devices with their start and end apart: 13, of which 6 were waited for; matrix products, arithmetic and copies ran while one was open for 0% of the time, Pallas kernels for 12%

profile of v4, /device:TPU:32, one launch (start us, length us, event | category | flops | bytes accessed | tf_op | source)
XLA Modules:
  0.0 91.2 jit_solution(6136120119913872572)
XLA Ops:
  0.6 1.2 %dynamic-slice_bitcast_fusion.1 = (f32[4,64,256]{2,1,0:T(8,128)S(1)}, f32[4,64,256]{2,1,0:T(8,128)S(1)}) fusion(f32[1,8,128,256]{3,2,1,0:T(8,128)} %param.7, s32[]{:T(128)S(6)} %select_n.7), kind=kLoop, calls=%fused_computation.1 | loop fusion | bytes 1048580 | tf_op jit(solution)/shard_map/dynamic_slice | solution.py:324
  1.8 10.3 %collective-permute-start = (f32[4,64,256]{2,1,0:T(8,128)S(1)}, f32[4,64,256]{2,1,0:T(8,128)S(1)}, u32[]{:S(2)}, u32[]{:S(2)}) collective-permute-start(f32[4,64,256]{2,1,0:T(8,128)S(1)} %get-tuple-element.48), channel_id=1, source_target_pairs={{1,2},{3,4},{5,6},{7,8},{9,10},{11,12},{13,14},{15,16},{17,18},{19... | collective-permute-start | bytes 786440 | tf_op jit(solution)/shard_map/ppermute | solution.py:321
  12.1 1.9 %collective-permute-start.1 = (f32[4,64,256]{2,1,0:T(8,128)S(1)}, f32[4,64,256]{2,1,0:T(8,128)S(1)}, u32[]{:S(2)}, u32[]{:S(2)}) collective-permute-start(f32[4,64,256]{2,1,0:T(8,128)S(1)} %get-tuple-element.47), channel_id=1, source_target_pairs={{1,2},{3,4},{5,6},{7,8},{9,10},{11,12},{13,14},{15,16},{17,18},{19... | collective-permute-start | bytes 786440 | tf_op jit(solution)/shard_map/ppermute | solution.py:321
  14.1 1.9 %collective-permute-start.2 = (f32[4,128,256]{2,1,0:T(8,128)S(1)}, f32[4,128,256]{2,1,0:T(8,128)S(1)}, u32[]{:S(2)}, u32[]{:S(2)}) collective-permute-start(f32[4,128,256]{2,1,0:T(8,128)S(1)} %dynamic-slice_bitcast_fusion), channel_id=1, source_target_pairs={{0,1},{1,0},{2,3},{3,2},{4,5},{5,4},{6,7},{7,6},{8,9},{9,8},{10,11... | collective-permute-start | bytes 1572872 | tf_op jit(solution)/shard_map/ppermute | solution.py:327
  16.0 1.2 %shard_map.85.total = f32[8,128,256]{2,1,0:T(8,128)S(1)} custom-call(f32[8,128,256]{2,1,0:T(8,128)S(1)} %bitcast.10), custom_call_target="tpu_custom_call" | custom-call | flops 1 | bytes 1 | tf_op jit(solution)/shard_map/pallas_call | solution.py:48
  17.2 0.3 copy-done.2
  17.6 0.4 copy-done.4
  18.0 1.5 %shard_map.86 = (f32[8,128,256]{2,1,0:T(8,128)S(1)}, f32[4,128,256]{2,1,0:T(8,128)S(1)}, f32[4,128,256]{2,1,0:T(8,128)S(1)}) custom-call(f32[16]{0:T(128)S(1)} %copy-done.4, f32[8,128,256]{2,1,0:T(8,128)S(1)} %bitcast.11, f32[8,128,256]{2,1,0:T(8,128)S(1)} %bitcast.13, s32[8,128,256]{2,1,0:T(8,128)S(1)} %copy-done.2, f32[8,128,256]{2,1,0:T(8,128)S(1)} %shard_map.85.total), custom_call_target="tpu_custom_call" | custom-call | flops 1 | bytes 1 | tf_op jit(solution)/shard_map/pallas_call | solution.py:48
  19.5 7.9 %collective-permute-start.3 = (f32[4,64,256]{2,1,0:T(8,128)S(1)}, f32[4,64,256]{2,1,0:T(8,128)S(1)}, u32[]{:S(2)}, u32[]{:S(2)}) collective-permute-start(f32[4,64,256]{2,1,0:T(8,128)S(1)} %shard_map.87.refs_1_.n1.refs_0_), channel_id=1, source_target_pairs={{1,2},{3,4},{5,6},{7,8},{9,10},{11,12},{13,14},{15,16},{17,18},{19... | collective-permute-start | bytes 786440 | tf_op jit(solution)/shard_map/ppermute | solution.py:321
  27.5 3.7 %collective-permute-start.4 = (f32[4,64,256]{2,1,0:T(8,128)S(1)}, f32[4,64,256]{2,1,0:T(8,128)S(1)}, u32[]{:S(2)}, u32[]{:S(2)}) collective-permute-start(f32[4,64,256]{2,1,0:T(8,128)S(1)} %get-tuple-element.28.n2.refs_1_), channel_id=1, source_target_pairs={{1,2},{3,4},{5,6},{7,8},{9,10},{11,12},{13,14},{15,16},{17,18},{19... | collective-permute-start | bytes 786440 | tf_op jit(solution)/shard_map/ppermute | solution.py:321
  31.3 1.4 %shard_map.89 = (f32[4,128,256]{2,1,0:T(8,128)S(1)}, f32[4,128,256]{2,1,0:T(8,128)S(1)}, f32[4,128,256]{2,1,0:T(8,128)S(1)}) custom-call(f32[4,64,256]{2,1,0:T(8,128)S(1)} %shard_map.87.refs_1_.n1.refs_0_, f32[4,64,256]{2,1,0:T(8,128)S(1)} %get-tuple-element.28.n2.refs_1_, f32[4,128,256]{2,1,0:T(8,128)S(1)} %get-tuple-element.29.partial, ...), custom_call_target="tpu_custom_call" | custom-call | flops 1 | bytes 1 | tf_op jit(solution)/shard_map/pallas_call | solution.py:48
  32.6 1.9 %collective-permute-start.5 = (f32[4,128,256]{2,1,0:T(8,128)S(1)}, f32[4,128,256]{2,1,0:T(8,128)S(1)}, u32[]{:S(2)}, u32[]{:S(2)}) collective-permute-start(f32[4,128,256]{2,1,0:T(8,128)S(1)} %get-tuple-element.34.refs_2_), channel_id=1, source_target_pairs={{0,1},{1,0},{2,3},{3,2},{4,5},{5,4},{6,7},{7,6},{8,9},{9,8},{10,11... | collective-permute-start | bytes 1572872 | tf_op jit(solution)/shard_map/ppermute | solution.py:377
  34.7 6.0 %collective-permute-start.6 = (f32[4,64,256]{2,1,0:T(8,128)S(1)}, f32[4,64,256]{2,1,0:T(8,128)S(1)}, u32[]{:S(2)}, u32[]{:S(2)}) collective-permute-start(f32[4,64,256]{2,1,0:T(8,128)S(1)} %shard_map.90.refs_1_.n1.refs_0_.refs_3_), channel_id=1, source_target_pairs={{1,2},{3,4},{5,6},{7,8},{9,10},{11,12},{13,14},{15,16},{17,18},{19... | collective-permute-start | bytes 786440 | tf_op jit(solution)/shard_map/ppermute | solution.py:321
  40.7 1.5 %collective-permute-done.4.halo = f32[4,64,256]{2,1,0:T(8,128)S(1)} collective-permute-done((f32[4,64,256]{2,1,0:T(8,128)S(1)}, f32[4,64,256]{2,1,0:T(8,128)S(1)}, u32[]{:S(2)}, u32[]{:S(2)}) %collective-permute-start.4) | collective-permute-done | bytes 262176 | tf_op jit(solution)/shard_map/ppermute | solution.py:321
  42.3 4.2 %collective-permute-start.7 = (f32[4,64,256]{2,1,0:T(8,128)S(1)}, f32[4,64,256]{2,1,0:T(8,128)S(1)}, u32[]{:S(2)}, u32[]{:S(2)}) collective-permute-start(f32[4,64,256]{2,1,0:T(8,128)S(1)} %get-tuple-element.32.n2.refs_1_.refs_4_), channel_id=1, source_target_pairs={{1,2},{3,4},{5,6},{7,8},{9,10},{11,12},{13,14},{15,16},{17,18},{19... | collective-permute-start | bytes 786440 | tf_op jit(solution)/shard_map/ppermute | solution.py:321
  46.6 1.3 %shard_map.92 = (f32[4,128,256]{2,1,0:T(8,128)S(1)}, f32[4,128,256]{2,1,0:T(8,128)S(1)}, f32[4,128,256]{2,1,0:T(8,128)S(1)}) custom-call(f32[4,64,256]{2,1,0:T(8,128)S(1)} %shard_map.90.refs_1_.n1.refs_0_.refs_3_, f32[4,64,256]{2,1,0:T(8,128)S(1)} %get-tuple-element.32.n2.refs_1_.refs_4_, f32[4,128,256]{2,1,0:T(8,128)S(1)} %get-tuple-element.33.partial, ...), custom_call_target="tpu_custom_call" | custom-call | flops 1 | bytes 1 | tf_op jit(solution)/shard_map/pallas_call | solution.py:48
  47.9 1.9 %collective-permute-start.8 = (f32[4,128,256]{2,1,0:T(8,128)S(1)}, f32[4,128,256]{2,1,0:T(8,128)S(1)}, u32[]{:S(2)}, u32[]{:S(2)}) collective-permute-start(f32[4,128,256]{2,1,0:T(8,128)S(1)} %get-tuple-element.39.refs_2_.refs_5_), channel_id=1, source_target_pairs={{0,1},{1,0},{2,3},{3,2},{4,5},{5,4},{6,7},{7,6},{8,9},{9,8},{10,11... | collective-permute-start | bytes 1572872 | tf_op jit(solution)/shard_map/ppermute | solution.py:377
  49.9 5.5 %collective-permute-start.9 = (f32[4,64,256]{2,1,0:T(8,128)S(1)}, f32[4,64,256]{2,1,0:T(8,128)S(1)}, u32[]{:S(2)}, u32[]{:S(2)}) collective-permute-start(f32[4,64,256]{2,1,0:T(8,128)S(1)} %shard_map.93.refs_1_.n1.refs_6_), channel_id=1, source_target_pairs={{1,2},{3,4},{5,6},{7,8},{9,10},{11,12},{13,14},{15,16},{17,18},{19... | collective-permute-start | bytes 786440 | tf_op jit(solution)/shard_map/ppermute | solution.py:321
  55.4 1.6 %collective-permute-done.7.halo = f32[4,64,256]{2,1,0:T(8,128)S(1)} collective-permute-done((f32[4,64,256]{2,1,0:T(8,128)S(1)}, f32[4,64,256]{2,1,0:T(8,128)S(1)}, u32[]{:S(2)}, u32[]{:S(2)}) %collective-permute-start.7) | collective-permute-done | bytes 262176 | tf_op jit(solution)/shard_map/ppermute | solution.py:321
  57.1 3.5 %collective-permute-start.10 = (f32[4,64,256]{2,1,0:T(8,128)S(1)}, f32[4,64,256]{2,1,0:T(8,128)S(1)}, u32[]{:S(2)}, u32[]{:S(2)}) collective-permute-start(f32[4,64,256]{2,1,0:T(8,128)S(1)} %get-tuple-element.37.n2.refs_7_), channel_id=1, source_target_pairs={{1,2},{3,4},{5,6},{7,8},{9,10},{11,12},{13,14},{15,16},{17,18},{19... | collective-permute-start | bytes 786440 | tf_op jit(solution)/shard_map/ppermute | solution.py:321
  60.7 1.3 %shard_map.95 = (f32[4,128,256]{2,1,0:T(8,128)S(1)}, f32[4,128,256]{2,1,0:T(8,128)S(1)}, f32[4,128,256]{2,1,0:T(8,128)S(1)}) custom-call(f32[4,64,256]{2,1,0:T(8,128)S(1)} %shard_map.93.refs_1_.n1.refs_6_, f32[4,64,256]{2,1,0:T(8,128)S(1)} %get-tuple-element.37.n2.refs_7_, f32[4,128,256]{2,1,0:T(8,128)S(1)} %get-tuple-element.38.partial, ...), custom_call_target="tpu_custom_call" | custom-call | flops 1 | bytes 1 | tf_op jit(solution)/shard_map/pallas_call | solution.py:48
  62.0 1.9 %collective-permute-start.11 = (f32[4,128,256]{2,1,0:T(8,128)S(1)}, f32[4,128,256]{2,1,0:T(8,128)S(1)}, u32[]{:S(2)}, u32[]{:S(2)}) collective-permute-start(f32[4,128,256]{2,1,0:T(8,128)S(1)} %get-tuple-element.40.na.refs_8_), channel_id=1, source_target_pairs={{0,1},{1,0},{2,3},{3,2},{4,5},{5,4},{6,7},{7,6},{8,9},{9,8},{10,11... | collective-permute-start | bytes 1572872 | tf_op jit(solution)/shard_map/ppermute | solution.py:377
  63.9 0.9 collective-permute-done.9.halo
  64.9 0.9 collective-permute-done.11.far_halo
  65.8 1.9 %shard_map.98 = (f32[4,128,256]{2,1,0:T(8,128)S(1)}, f32[8,4,8,8,128]{4,3,2,1,0:T(8,128)}) custom-call(f32[2,8,128]{2,1,0:T(8,128)S(1)} %broadcast_in_dim.13.box_ref, f32[8,128,256]{2,1,0:T(8,128)S(1)} %get-tuple-element.26.coef.refs_1_.refs_3_, f32[4,128,256]{2,1,0:T(8,128)S(1)} %get-tuple-element.42.partial, ...), custom_call_target="tpu_custom_call" | custom-call | flops 1 | bytes 1 | tf_op jit(solution)/shard_map/pallas_call | solution.py:48
  67.8 3.7 %collective-permute-done.10.halo = f32[4,64,256]{2,1,0:T(8,128)S(1)} collective-permute-done((f32[4,64,256]{2,1,0:T(8,128)S(1)}, f32[4,64,256]{2,1,0:T(8,128)S(1)}, u32[]{:S(2)}, u32[]{:S(2)}) %collective-permute-start.10) | collective-permute-done | bytes 262176 | tf_op jit(solution)/shard_map/ppermute | solution.py:321
  71.5 1.0 %shard_map.99 = (f32[4,64,256]{2,1,0:T(8,128)S(1)}, f32[8,4,8,8,128]{4,3,2,1,0:T(8,128)}) custom-call(f32[2,8,128]{2,1,0:T(8,128)S(1)} %broadcast_in_dim.13.box_ref, f32[4,128,256]{2,1,0:T(8,128)S(1)} %get-tuple-element.41.base, f32[8,128,256]{2,1,0:T(8,128)S(1)} %get-tuple-element.26.coef.refs_1_.refs_3_, ...), custom_call_target="tpu_custom_call", output_to_operand_aliasing={{1}: (5, {})} | custom-call | flops 1 | bytes 1 | tf_op jit(solution)/shard_map/pallas_call | solution.py:48
  72.5 4.4 %all-to-all-start = ((f32[8,4,8,8,128]{4,3,2,1,0:T(8,128)}), f32[8,4,8,8,128]{4,3,2,1,0:T(8,128)S(1)}, u32[]{:S(2)}, u32[]{:S(2)}) async-start(f32[8,4,8,8,128]{4,3,2,1,0:T(8,128)} %get-tuple-element.46), calls=%async_computation | async-start | bytes 2097152 | tf_op jit(solution)/shard_map/all_to_all | solution.py:407
  77.0 1.1 %shard_map.96 = f32[8,128,256]{2,1,0:T(8,128)} custom-call(f32[4,64,256]{2,1,0:T(8,128)S(1)} %shard_map.93.refs_1_.n1.refs_6_, f32[4,64,256]{2,1,0:T(8,128)S(1)} %get-tuple-element.37.n2.refs_7_, f32[4,128,256]{2,1,0:T(8,128)S(1)} %get-tuple-element.40.na.refs_8_), custom_call_target="tpu_custom_call" | custom-call | flops 1 | bytes 1 | tf_op jit(solution)/shard_map/pallas_call | solution.py:48
  78.0 1.1 %shard_map.100 = f32[8,128,256]{2,1,0:T(8,128)} custom-call(f32[4,64,256]{2,1,0:T(8,128)S(1)} %shard_map.97.n1, f32[4,64,256]{2,1,0:T(8,128)S(1)} %get-tuple-element.44.n2, f32[4,128,256]{2,1,0:T(8,128)S(1)} %get-tuple-element.45.na), custom_call_target="tpu_custom_call" | custom-call | flops 1 | bytes 1 | tf_op jit(solution)/shard_map/pallas_call | solution.py:48
  79.1 11.4 %all-to-all-done.received = f32[8,4,8,8,128]{4,3,2,1,0:T(8,128)S(1)} async-done(((f32[8,4,8,8,128]{4,3,2,1,0:T(8,128)}), f32[8,4,8,8,128]{4,3,2,1,0:T(8,128)S(1)}, u32[]{:S(2)}, u32[]{:S(2)}) %all-to-all-start) | async-done | bytes 1048608 | tf_op jit(solution)/shard_map/all_to_all | solution.py:407
  90.5 0.7 shard_map.101
  (27 shorter events, 0.7 us)
Async XLA Ops:
  0.6 13.4 %copy-start = (f32[1,8,128,256]{3,2,1,0:T(8,128)S(1)}, f32[1,8,128,256]{3,2,1,0:T(8,128)}, u32[]{:S(2)}) copy-start(f32[1,8,128,256]{3,2,1,0:T(8,128)} %param.7) | copy-start | bytes 3145732
  1.8 17.6 %collective-permute-start = (f32[4,64,256]{2,1,0:T(8,128)S(1)}, f32[4,64,256]{2,1,0:T(8,128)S(1)}, u32[]{:S(2)}, u32[]{:S(2)}) collective-permute-start(f32[4,64,256]{2,1,0:T(8,128)S(1)} %get-tuple-element.48), channel_id=1, source_target_pairs={{1,2},{3,4},{5,6},{7,8},{9,10},{11,12},{13,14},{15,16},{17,18},{19... | collective-permute-start | bytes 786440 | tf_op jit(solution)/shard_map/ppermute | solution.py:321
  12.1 15.3 %collective-permute-start.1 = (f32[4,64,256]{2,1,0:T(8,128)S(1)}, f32[4,64,256]{2,1,0:T(8,128)S(1)}, u32[]{:S(2)}, u32[]{:S(2)}) collective-permute-start(f32[4,64,256]{2,1,0:T(8,128)S(1)} %get-tuple-element.47), channel_id=1, source_target_pairs={{1,2},{3,4},{5,6},{7,8},{9,10},{11,12},{13,14},{15,16},{17,18},{19... | collective-permute-start | bytes 786440 | tf_op jit(solution)/shard_map/ppermute | solution.py:321
  14.1 17.2 %collective-permute-start.2 = (f32[4,128,256]{2,1,0:T(8,128)S(1)}, f32[4,128,256]{2,1,0:T(8,128)S(1)}, u32[]{:S(2)}, u32[]{:S(2)}) collective-permute-start(f32[4,128,256]{2,1,0:T(8,128)S(1)} %dynamic-slice_bitcast_fusion), channel_id=1, source_target_pairs={{0,1},{1,0},{2,3},{3,2},{4,5},{5,4},{6,7},{7,6},{8,9},{9,8},{10,11... | collective-permute-start | bytes 1572872 | tf_op jit(solution)/shard_map/ppermute | solution.py:327
  16.0 1.2 %copy-start.1 = (f32[1,8,128,256]{3,2,1,0:T(8,128)S(1)}, f32[1,8,128,256]{3,2,1,0:T(8,128)}, u32[]{:S(2)}) copy-start(f32[1,8,128,256]{3,2,1,0:T(8,128)} %param.6) | copy-start | bytes 3145732
  16.0 1.5 %copy-start.2 = (s32[8,128,256]{2,1,0:T(8,128)S(1)}, s32[8,128,256]{2,1,0:T(8,128)}, u32[]{:S(2)}) copy-start(s32[8,128,256]{2,1,0:T(8,128)} %regions.1) | copy-start | bytes 3145732
  17.2 0.7 copy-start.4
  19.5 15.0 %collective-permute-start.3 = (f32[4,64,256]{2,1,0:T(8,128)S(1)}, f32[4,64,256]{2,1,0:T(8,128)S(1)}, u32[]{:S(2)}, u32[]{:S(2)}) collective-permute-start(f32[4,64,256]{2,1,0:T(8,128)S(1)} %shard_map.87.refs_1_.n1.refs_0_), channel_id=1, source_target_pairs={{1,2},{3,4},{5,6},{7,8},{9,10},{11,12},{13,14},{15,16},{17,18},{19... | collective-permute-start | bytes 786440 | tf_op jit(solution)/shard_map/ppermute | solution.py:321
  27.5 14.7 %collective-permute-start.4 = (f32[4,64,256]{2,1,0:T(8,128)S(1)}, f32[4,64,256]{2,1,0:T(8,128)S(1)}, u32[]{:S(2)}, u32[]{:S(2)}) collective-permute-start(f32[4,64,256]{2,1,0:T(8,128)S(1)} %get-tuple-element.28.n2.refs_1_), channel_id=1, source_target_pairs={{1,2},{3,4},{5,6},{7,8},{9,10},{11,12},{13,14},{15,16},{17,18},{19... | collective-permute-start | bytes 786440 | tf_op jit(solution)/shard_map/ppermute | solution.py:321
  32.6 13.9 %collective-permute-start.5 = (f32[4,128,256]{2,1,0:T(8,128)S(1)}, f32[4,128,256]{2,1,0:T(8,128)S(1)}, u32[]{:S(2)}, u32[]{:S(2)}) collective-permute-start(f32[4,128,256]{2,1,0:T(8,128)S(1)} %get-tuple-element.34.refs_2_), channel_id=1, source_target_pairs={{0,1},{1,0},{2,3},{3,2},{4,5},{5,4},{6,7},{7,6},{8,9},{9,8},{10,11... | collective-permute-start | bytes 1572872 | tf_op jit(solution)/shard_map/ppermute | solution.py:377
  34.7 15.2 %collective-permute-start.6 = (f32[4,64,256]{2,1,0:T(8,128)S(1)}, f32[4,64,256]{2,1,0:T(8,128)S(1)}, u32[]{:S(2)}, u32[]{:S(2)}) collective-permute-start(f32[4,64,256]{2,1,0:T(8,128)S(1)} %shard_map.90.refs_1_.n1.refs_0_.refs_3_), channel_id=1, source_target_pairs={{1,2},{3,4},{5,6},{7,8},{9,10},{11,12},{13,14},{15,16},{17,18},{19... | collective-permute-start | bytes 786440 | tf_op jit(solution)/shard_map/ppermute | solution.py:321
  42.3 4.3 %copy-start.5 = (s32[2]{0:T(128)S(1)}, s32[2]{0:T(128)}, u32[]{:S(2)}) copy-start(s32[2]{0:T(128)} %param.11) | copy-start | bytes 28
  42.3 14.8 %collective-permute-start.7 = (f32[4,64,256]{2,1,0:T(8,128)S(1)}, f32[4,64,256]{2,1,0:T(8,128)S(1)}, u32[]{:S(2)}, u32[]{:S(2)}) collective-permute-start(f32[4,64,256]{2,1,0:T(8,128)S(1)} %get-tuple-element.32.n2.refs_1_.refs_4_), channel_id=1, source_target_pairs={{1,2},{3,4},{5,6},{7,8},{9,10},{11,12},{13,14},{15,16},{17,18},{19... | collective-permute-start | bytes 786440 | tf_op jit(solution)/shard_map/ppermute | solution.py:321
  47.9 12.8 %collective-permute-start.8 = (f32[4,128,256]{2,1,0:T(8,128)S(1)}, f32[4,128,256]{2,1,0:T(8,128)S(1)}, u32[]{:S(2)}, u32[]{:S(2)}) collective-permute-start(f32[4,128,256]{2,1,0:T(8,128)S(1)} %get-tuple-element.39.refs_2_.refs_5_), channel_id=1, source_target_pairs={{0,1},{1,0},{2,3},{3,2},{4,5},{5,4},{6,7},{7,6},{8,9},{9,8},{10,11... | collective-permute-start | bytes 1572872 | tf_op jit(solution)/shard_map/ppermute | solution.py:377
  49.9 14.9 %collective-permute-start.9 = (f32[4,64,256]{2,1,0:T(8,128)S(1)}, f32[4,64,256]{2,1,0:T(8,128)S(1)}, u32[]{:S(2)}, u32[]{:S(2)}) collective-permute-start(f32[4,64,256]{2,1,0:T(8,128)S(1)} %shard_map.93.refs_1_.n1.refs_6_), channel_id=1, source_target_pairs={{1,2},{3,4},{5,6},{7,8},{9,10},{11,12},{13,14},{15,16},{17,18},{19... | collective-permute-start | bytes 786440 | tf_op jit(solution)/shard_map/ppermute | solution.py:321
  57.1 14.4 %collective-permute-start.10 = (f32[4,64,256]{2,1,0:T(8,128)S(1)}, f32[4,64,256]{2,1,0:T(8,128)S(1)}, u32[]{:S(2)}, u32[]{:S(2)}) collective-permute-start(f32[4,64,256]{2,1,0:T(8,128)S(1)} %get-tuple-element.37.n2.refs_7_), channel_id=1, source_target_pairs={{1,2},{3,4},{5,6},{7,8},{9,10},{11,12},{13,14},{15,16},{17,18},{19... | collective-permute-start | bytes 786440 | tf_op jit(solution)/shard_map/ppermute | solution.py:321
  62.0 3.8 %collective-permute-start.11 = (f32[4,128,256]{2,1,0:T(8,128)S(1)}, f32[4,128,256]{2,1,0:T(8,128)S(1)}, u32[]{:S(2)}, u32[]{:S(2)}) collective-permute-start(f32[4,128,256]{2,1,0:T(8,128)S(1)} %get-tuple-element.40.na.refs_8_), channel_id=1, source_target_pairs={{0,1},{1,0},{2,3},{3,2},{4,5},{5,4},{6,7},{7,6},{8,9},{9,8},{10,11... | collective-permute-start | bytes 1572872 | tf_op jit(solution)/shard_map/ppermute | solution.py:377
  72.5 18.0 %all-to-all-start = ((f32[8,4,8,8,128]{4,3,2,1,0:T(8,128)}), f32[8,4,8,8,128]{4,3,2,1,0:T(8,128)S(1)}, u32[]{:S(2)}, u32[]{:S(2)}) async-start(f32[8,4,8,8,128]{4,3,2,1,0:T(8,128)} %get-tuple-element.46), calls=%async_computation | async-start | bytes 2097152 | tf_op jit(solution)/shard_map/all_to_all | solution.py:407
  78.0 12.5 %copy-start.3 = (f32[8,8,128]{2,1,0:T(8,128)S(1)}, f32[8,8,128]{2,1,0:T(8,128)}, u32[]{:S(2)}) copy-start(f32[8,8,128]{2,1,0:T(8,128)} %image.1) | copy-start | bytes 98308
